TPU v7x, 256 devices: a whole 4x4x8 slice. The times are simulated.
256 devices in a mesh: row: 32 (over x_hi, z, core), col: 8 (over y, x_lo).
Axes of the slice: x: 4 (x_hi: 2, x_lo: 2; x = x_hi * 2 + x_lo), y: 4, z: 8, core: 2. Of those that a mesh axis runs over, the one named last changes fastest.
Arguments:
- features: bfloat16 [8, 8192, 128], P('col', 'row'), may hold values from -6 to 6
- tiles: bfloat16 [32, 8, 256, 128, 128], P('row', 'col'), may hold values from -0.15625 to 0.15625
- tile_rows: int32 [32, 8, 256], P('row', 'col'), may hold values from 0 to 15
- tile_cols: int32 [32, 8, 256], P('row', 'col'), may hold values from 0 to 63
- tile_count: int32 [32, 8], P('row', 'col'), may hold values from 32 to 256, as said below
- weight: bfloat16 [128, 128], replicated, may hold values from -0.5 to 0.5
- grad_out: bfloat16 [32, 2048, 128], P('row', 'col'), may hold values from -6 to 6
Outputs:
- layer_out: bfloat16 [32, 2048, 128], P('row', 'col')
- grad_features: bfloat16 [8, 8192, 128], P('col', 'row')
- grad_weight: float32 [128, 128], replicated
Inputs may be any that keep to these rules, and one draw needn't show every extreme that they name: tile_count[r, c] slots of device (r, c), the first ones of its list, are live; the rest are ignored. Some device holds 256 live tiles in every draw.
All inputs are finite; a program needn't handle non-finite values.
Results may differ from a plain program's by a relative error of at most 0.022.
Values may be sent and summed in bfloat16 or wider, within the bound.
A program may use at most 128 MiB of HBM per device.

v0:
```python
import math

import jax
import jax.numpy as jnp
from jax import lax
from jax.sharding import PartitionSpec as P


def slot_products(tile_slots, picked, live_mask, pattern):
    product = jnp.einsum(pattern, tile_slots, picked, preferred_element_type=jnp.float32)
    product = product * live_mask.astype(jnp.float32)[:, None, None]
    flat = product.reshape(product.shape[0], -1)
    upper = flat.astype(jnp.bfloat16)
    lower = (flat - upper.astype(jnp.float32)).astype(jnp.bfloat16)
    return (upper, lower, product.shape[1], product.shape[2])


def select_blocks(parts, slot_index, block_total):
    upper, lower, side, width = parts
    targets = jnp.arange(block_total)
    selector = (slot_index[None, :] == targets[:, None]).astype(jnp.bfloat16)
    summed = jnp.dot(selector, upper, preferred_element_type=jnp.float32)
    summed = summed + jnp.dot(selector, lower, preferred_element_type=jnp.float32)
    return summed.reshape(block_total * side, width)


def per_device(features, tiles, tile_rows, tile_cols, tile_count, weight, grad_out):
    tile_slots = tiles[0, 0]
    slot_rows = tile_rows[0, 0]
    slot_cols = tile_cols[0, 0]
    side = tile_slots.shape[-1]
    width = features.shape[-1]
    piece_rows = features.shape[1]
    own_blocks = piece_rows // side
    row_size = lax.axis_size("row")
    col_size = lax.axis_size("col")
    live_mask = jnp.arange(tile_slots.shape[0]) < tile_count[0, 0]
    column_group = lax.all_gather(features, "row", axis=1, tiled=True)[0]
    column_blocks = column_group.reshape(-1, side, width)
    picked = column_blocks[slot_cols]
    forward_parts = slot_products(tile_slots, picked, live_mask, "sij,sjf->sif")
    partial_value = select_blocks(forward_parts, slot_rows, own_blocks * col_size)
    own_share = lax.psum_scatter(
        partial_value.astype(jnp.bfloat16), "col", scatter_dimension=0, tiled=True
    )
    layer_out = jnp.dot(own_share, weight, preferred_element_type=jnp.float32).astype(jnp.bfloat16)
    grad_local = grad_out[0]
    weight_term = lax.dot_general(
        own_share, grad_local, (((0,), (0,)), ((), ())), preferred_element_type=jnp.float32
    )
    node_total = piece_rows * row_size * col_size
    grad_weight = lax.psum(weight_term, ("row", "col")) / math.sqrt(node_total)
    grad_agg = lax.dot_general(
        grad_local, weight, (((1,), (1,)), ((), ())), preferred_element_type=jnp.float32
    )
    grad_agg = grad_agg.astype(jnp.bfloat16)
    row_group = lax.all_gather(grad_agg, "col", axis=0, tiled=True)
    row_blocks = row_group.reshape(-1, side, width)
    picked_grad = row_blocks[slot_rows]
    backward_parts = slot_products(tile_slots, picked_grad, live_mask, "sij,sif->sjf")
    back_partial = select_blocks(backward_parts, slot_cols, own_blocks * row_size)
    back_share = lax.psum_scatter(
        back_partial.astype(jnp.bfloat16), "row", scatter_dimension=0, tiled=True
    )
    return (layer_out[None], back_share[None], grad_weight)


def solution(mesh):
    in_specs = (
        P("col", "row", None),
        P("row", "col", None, None, None),
        P("row", "col", None),
        P("row", "col", None),
        P("row", "col"),
        P(),
        P("row", "col", None),
    )
    out_specs = (P("row", "col", None), P("col", "row", None), P())
    return jax.shard_map(
        per_device, mesh=mesh, in_specs=in_specs, out_specs=out_specs, check_vma=False
    )
```

profile of v0, /device:TPU:1, one launch (start us, length us, event | category | flops | bytes accessed | tf_op | source)
XLA Modules:
  0.0 551.1 jit_solution(14463223209952672529)
XLA Ops:
  8.6 0.7 compare_select_fusion
  9.3 0.9 convolution_convert_fusion
  10.2 26.1 %all_gather.7 = bf16[2048,128]{1,0:T(8,128)(2,1)S(1)} all-gather(bf16[256,128]{1,0:T(8,128)(2,1)S(1)} %convolution_convert_fusion), channel_id=1, replica_groups=mesh['row'=32,'col'=8] {'col'}, dimensions={0}, use_global_device_ids=true | all-gather | bytes 589824 | tf_op jit(solution)/shard_map/all_gather | solution.py:57
  36.4 8.6 %gather_fusion.1 = bf16[256,128,128]{2,1,0:T(8,128)(2,1)} fusion(bf16[16,128,128]{2,1,0:T(8,128)(2,1)S(1)} %bitcast.51, s32[1024]{0:T(1024)S(1)} %pad_clamp_fusion), kind=kCustom, calls=%fused_computation.1 | custom fusion | bytes 16778240 | tf_op jit(solution)/shard_map/gather | solution.py:59
  45.0 15.4 %multiply_bitcast_fusion = f32[256,128,128]{1,2,0:T(8,128)} fusion(bf16[256,128,128]{2,1,0:T(8,128)(2,1)} %gather_fusion.1, bf16[1,1,256,128,128]{4,3,2,1,0:T(8,128)(2,1)} %param.8, f32[256]{0:T(256)S(1)} %compare_convert_fusion), kind=kOutput, calls=%fused_computation.12 | convolution fusion | flops 1077936128 | bytes 33555456 | tf_op jit(solution)/shard_map/sij,sif->sjf/dot_general | solution.py:10
  60.4 17.8 %copy.13 = f32[256,128,128]{0,2,1:T(8,128)} copy(f32[256,128,128]{1,2,0:T(8,128)} %multiply_bitcast_fusion) | data formatting | bytes 33554432 | tf_op jit(solution)/shard_map/mul | solution.py:11
  78.2 16.8 %all-gather.2.cloned.1.call-done = bf16[1,8192,128]{2,1,0:T(8,128)(2,1)} async-done(((bf16[1,256,128]{2,1,0:T(8,128)(2,1)}), bf16[1,8192,128]{2,1,0:T(8,128)(2,1)}) %all-gather.2.cloned.1.call-update) | async-done | bytes 2097168 | tf_op jit(solution)/shard_map/all_gather | solution.py:38
  95.0 10.2 %gather_fusion = bf16[256,128,128]{2,1,0:T(8,128)(2,1)} fusion(bf16[64,128,128]{2,1,0:T(8,128)(2,1)} %bitcast.52, s32[1024]{0:T(1024)S(1)} %pad_clamp_fusion.1), kind=kCustom, calls=%fused_computation | custom fusion | bytes 16778240 | tf_op jit(solution)/shard_map/gather | solution.py:40
  105.1 13.0 %multiply_bitcast_fusion.1 = f32[256,128,128]{1,2,0:T(8,128)} fusion(bf16[256,128,128]{2,1,0:T(8,128)(2,1)} %gather_fusion, bf16[1,1,256,128,128]{4,3,2,1,0:T(8,128)(2,1)} %param.8, f32[256]{0:T(256)S(1)} %compare_convert_fusion), kind=kOutput, calls=%fused_computation.13 | convolution fusion | flops 1077936128 | bytes 33555456 | tf_op jit(solution)/shard_map/sij,sjf->sif/dot_general | solution.py:10
  118.1 17.8 %copy.11 = f32[256,128,128]{0,2,1:T(8,128)} copy(f32[256,128,128]{1,2,0:T(8,128)} %multiply_bitcast_fusion.1) | data formatting | bytes 33554432 | tf_op jit(solution)/shard_map/mul | solution.py:11
  135.9 6.9 %fusion.3 = (bf16[256,16384]{0,1:T(8,128)(2,1)S(1)}, bf16[256,16384]{0,1:T(8,128)(2,1)S(1)}) fusion(f32[256,128,128]{0,2,1:T(8,128)} %copy.11), kind=kLoop, calls=%fused_computation.11 | loop fusion | flops 16777216 | bytes 33554432 | tf_op jit(solution)/shard_map/convert_element_type | solution.py:14
  142.8 2.3 fusion.13
  145.1 2.3 fusion.1
  147.4 1.1 convert_element_type.51
  148.5 9.4 %fusion.2 = (bf16[256,16384]{0,1:T(8,128)(2,1)}, bf16[256,16384]{0,1:T(8,128)(2,1)S(1)}) fusion(f32[256,128,128]{0,2,1:T(8,128)} %copy.13), kind=kLoop, calls=%fused_computation.8 | loop fusion | flops 16777216 | bytes 33554432 | tf_op jit(solution)/shard_map/convert_element_type | solution.py:14
  157.9 4.6 fusion.10
  162.5 18.3 %reduce-scatter.3.cloned.1.call-done = bf16[256,128]{1,0:T(8,128)(2,1)} async-done(((bf16[2048,128]{1,0:T(8,128)(2,1)}), bf16[256,128]{1,0:T(8,128)(2,1)}) %reduce-scatter.3.cloned.1.call-update) | async-done | bytes 65552 | tf_op jit(solution)/shard_map/reduce_scatter | solution.py:43
  180.8 1.7 fusion.7
  182.5 7.2 %fusion = bf16[64,16384]{1,0:T(8,128)(2,1)S(1)} fusion(f32[64,16384]{1,0:T(8,128)} %fusion.10, bf16[256,16384]{0,1:T(8,128)(2,1)} %get-tuple-element.3, s32[256]{0:T(256)S(1)} %bitcast.56), kind=kOutput, calls=%fused_computation.3 | convolution fusion | flops 538984448 | bytes 14681088 | tf_op jit(solution)/shard_map/dot_general | solution.py:23
  189.8 2.3 convert_element_type.58
  192.2 0.8 fusion.6
  192.9 236.2 %all-reduce.2.cloned.1.call-done = f32[128,128]{1,0:T(8,128)} async-done(((f32[128,128]{1,0:T(8,128)}), f32[128,128]{1,0:T(8,128)}) %all-reduce.2.cloned.1.call-update) | async-done | bytes 65552 | tf_op jit(solution)/shard_map/psum | solution.py:52
  429.2 1.5 broadcast_multiply_fusion
  430.6 113.9 %reduce-scatter.5.cloned.1.call-done = bf16[256,128]{1,0:T(8,128)(2,1)} async-done(((bf16[8192,128]{1,0:T(8,128)(2,1)}), bf16[256,128]{1,0:T(8,128)(2,1)}) %reduce-scatter.5.cloned.1.call-update) | async-done | bytes 65552 | tf_op jit(solution)/shard_map/reduce_scatter | solution.py:62
  (22 shorter events, 0.9 us)
Async XLA Ops:
  7.2 2.1 copy-start
  7.2 87.8 %all-gather.2.cloned.1.call-start = ((), (), s32[]{:S(2)}) async-start(), calls=%async_computation.2 | async-start | bytes 2162688 | tf_op jit(solution)/shard_map/all_gather | solution.py:38
  7.9 172.9 %reduce-scatter.3.cloned.1.call-start = ((), (), s32[]{:S(2)}) async-start(), calls=%async_computation.3 | async-start | bytes 589824 | tf_op jit(solution)/shard_map/reduce_scatter | solution.py:43
  60.4 17.8 %copy-start.4 = (s32[1,1,256]{2,1,0:T(1,128)S(1)}, s32[1,1,256]{2,1,0:T(1,128)}, u32[]{:S(2)}) copy-start(s32[1,1,256]{2,1,0:T(1,128)} %param.10) | copy-start | bytes 3076
  135.9 6.9 %copy-start.3 = (s32[1,1,256]{2,1,0:T(1,128)S(1)}, s32[1,1,256]{2,1,0:T(1,128)}, u32[]{:S(2)}) copy-start(s32[1,1,256]{2,1,0:T(1,128)} %param.9) | copy-start | bytes 3076
  148.5 280.7 %all-reduce.2.cloned.1.call-start = ((), (), s32[]{:S(2)}) async-start(), calls=%async_computation.5 | async-start | bytes 131072 | tf_op jit(solution)/shard_map/psum | solution.py:52
  182.5 362.1 %reduce-scatter.5.cloned.1.call-start = ((), (), s32[]{:S(2)}) async-start(), calls=%async_computation.4 | async-start | bytes 2162688 | tf_op jit(solution)/shard_map/reduce_scatter | solution.py:62
  182.5 9.6 %copy-start.1 = (bf16[256,128]{1,0:T(8,128)(2,1)S(1)}, bf16[256,128]{1,0:T(8,128)(2,1)}, u32[]{:S(2)}) copy-start(bf16[256,128]{1,0:T(8,128)(2,1)} %reduce-scatter.3.cloned.1.call-done) | copy-start | bytes 196612
  182.5 9.6 %copy-start.2 = (bf16[128,128]{1,0:T(8,128)(2,1)S(1)}, bf16[128,128]{1,0:T(8,128)(2,1)}, u32[]{:S(2)}) copy-start(bf16[128,128]{1,0:T(8,128)(2,1)} %param.12) | copy-start | bytes 98308
Sparse Core Ops, SparseCore 0:
  10.8 84.1 all-gather.1
  148.6 32.1 reduce-scatter.2
  187.8 241.3 all-reduce.1
  434.3 110.1 reduce-scatter.4
where the time goes:
time: 556 us; the launch traced here: 551 us
  waiting for transfers between devices  386 us (69%)
  local copies, waits for them, and re-layouts  57.8 us (10%)
  matrix products  48.2 us (9%)
  blocking collectives  26.1 us (5%)
  other arithmetic  18.4 us (3%)
  between operations  14.5 us (3%)
    psum x1, waiting for transfers between devices, per_device(): grad_weight = lax.psum(weight_term, ('row', 'col')) / math.sqrt(node_total)  236 us
    reduce_scatter x1, waiting for transfers between devices, per_device(): lax.psum_scatter(back_partial.astype(jnp.bfloat16), 'row', scatter_dimens...  114 us
    mul x2, local copies, waits for them, and re-layouts, slot_products(): product = product * live_mask.astype(jnp.float32)[:, None, None]  35.6 us
    dot_general x2, matrix products, slot_products(): jnp.einsum(pattern, tile_slots, picked, preferred_element_type=jnp.float32)  28.4 us
    all_gather x1, blocking collectives, per_device(): row_group = lax.all_gather(grad_agg, 'col', axis=0, tiled=True)  26.1 us
    reduce_scatter x1, waiting for transfers between devices, per_device(): lax.psum_scatter(partial_value.astype(jnp.bfloat16), 'col', scatter_dimen...  18.3 us
    all_gather x1, waiting for transfers between devices, per_device(): column_group = lax.all_gather(features, 'row', axis=1, tiled=True)[0]  16.8 us
    convert_element_type x2, other arithmetic, slot_products(): lower = (flat - upper.astype(jnp.float32)).astype(jnp.bfloat16)  16.3 us
  transfers between devices with their start and end apart: 4, of which 4 were waited for; matrix products, arithmetic and copies ran while one was open for 13% of the time, Pallas kernels for 0%

commit v1 on v0

v1 whole, which is shorter than its diff:
```python
import math

import jax
import jax.numpy as jnp
from jax import lax
from jax.experimental import pallas as pl
from jax.experimental.pallas import tpu as pltpu
from jax.sharding import PartitionSpec as P

TB = 128
F = 128
SLOTS = 256
ROW_BLOCKS = 16
COL_BLOCKS = 64
NZ = 8
NCOL = 8
UNROLL = 32
STEPS = SLOTS // UNROLL
EMPTY = SLOTS
B_ORDER, B_LAST = 0, 256
F_ORDER, F_LAST = 320, 576
PLAN = 592
PIECES = ((0, 1), (1, 2), (3, 2), (5, 2), (7, 1))


def tile_plan(rows, cols, count):
    slot = jnp.arange(SLOTS, dtype=jnp.int32)
    live = slot < count
    key = jnp.stack([jnp.where(live, cols, 64), jnp.where(live, rows, 64)])
    other = jnp.stack([rows, cols])
    value = key * 65536 + slot[None, :] * 256 + other
    place = jnp.sum(value[:, None, :] < value[:, :, None], axis=2, dtype=jnp.int32)
    hit = place[:, None, :] == slot[None, :, None]
    order = jnp.sum(jnp.where(hit, value[:, None, :], 0), axis=2, dtype=jnp.int32)
    block = jnp.arange(COL_BLOCKS, dtype=jnp.int32)
    upto = jnp.sum(key[:, None, :] <= block[None, :, None], axis=2, dtype=jnp.int32)
    some = jnp.any(key[:, None, :] == block[None, :, None], axis=2)
    last = jnp.where(some, upto - 1, EMPTY)
    return jnp.concatenate([order[0], last[0], order[1], last[1, :ROW_BLOCKS]])


def remote(src, dst, send, recv, device):
    return pltpu.make_async_remote_copy(
        src_ref=src, dst_ref=dst, send_sem=send, recv_sem=recv,
        device_id=device, device_id_type=pl.DeviceIdType.MESH,
    )


def kernel(
    plan, feat, gout, w, tiles_hbm, lay_ref, gf_ref, gw_ref,
    tv, fbuf, gbuf, gagg, runs, part, peer, ring_out, ring_in, x_out, x_in,
    agg, agg_in, wt, red1, red2, red3, red4,
    tile_sem, col_s, col_r, agz_s, agz_r, agx, agp_s, agp_r,
    rp_s, rp_r, rz_s, rz_r, rx, cr_s, cr_r,
    a1_s, a1_r, a2_s, a2_r, a3_s, a3_r, a4_s, a4_r,
):
    r = lax.axis_index("row")
    c = lax.axis_index("col")
    core = lax.rem(r, 2)
    z = lax.rem(r // 2, NZ)
    xh = r // (2 * NZ)

    def rid(a, b, k):
        return (a * NZ + b) * 2 + k

    def zrel(o):
        return lax.rem(z + (o % NZ), NZ)

    def crel(o):
        return lax.rem(c + (o % NCOL), NCOL)

    up = (rid(xh, zrel(1), core), c)
    down = (rid(xh, zrel(-1), core), c)
    partner = (rid(xh, z, 1 - core), c)
    opposite = (rid(1 - xh, z, core), c)
    diagonal = (rid(1 - xh, z, 1 - core), c)
    zpeer = [None] + [(rid(xh, zrel(i), core), c) for i in range(1, NZ)]
    cpeer = [None] + [(r, crel(i)) for i in range(1, NCOL)]

    tile_copies = [
        pltpu.make_async_copy(
            tiles_hbm.at[pl.ds(64 * i, 64)], tv.at[pl.ds(64 * i, 64)], tile_sem.at[i]
        )
        for i in range(4)
    ]
    for copy in tile_copies:
        copy.start()
    barrier = pltpu.get_barrier_semaphore()
    everyone = zpeer[1:] + cpeer[1:] + [partner, opposite, diagonal]
    for device in everyone:
        pl.semaphore_signal(
            barrier, inc=1, device_id=device, device_id_type=pl.DeviceIdType.MESH
        )
    fbuf[pl.ds(2 * r, 2)] = feat[...]
    gbuf[pl.ds(2 * c, 2)] = gout[...]
    runs[EMPTY] = jnp.zeros((TB, F), jnp.float32)
    pl.semaphore_wait(barrier, len(everyone))

    def col_copy(i, owner):
        here = gbuf.at[pl.ds(2 * owner, 2)]
        return remote(here, here, col_s.at[i - 1], col_r.at[i - 1], cpeer[i])

    for i in range(1, NCOL):
        col_copy(i, c).start()

    def shard(st, o):
        return 2 * rid(xh if st == 0 else 1 - xh, zrel(o), core)

    def z_copy(st, way, step, first, size):
        here = fbuf.at[pl.ds(first, size)]
        return remote(
            here, here, agz_s.at[st, way, step], agz_r.at[st, way, step], up if way == 0 else down
        )

    def p_copy(st, o, mine=True):
        k = core if mine else 1 - core
        first = 2 * rid(xh if st == 0 else 1 - xh, zrel(o), k)
        here = fbuf.at[pl.ds(first, 2)]
        return remote(here, here, agp_s.at[st, o % NZ], agp_r.at[st, o % NZ], partner)

    def x_copy(first):
        here = fbuf.at[pl.ds(first, 2)]
        return remote(here, here, agx.at[0], agx.at[1], opposite)

    x_copy(2 * r).start()
    for way in range(2):
        z_copy(0, way, 0, 2 * r, 2).start()
    p_copy(0, 0).start()

    def gather_x():
        first = shard(1, 0)
        x_copy(first).wait_recv()
        for way in range(2):
            z_copy(1, way, 0, first, 2).start()
        p_copy(1, 0).start()

    def gather_step(st, s):
        for way in range(2):
            o = -s if way == 0 else s
            first = shard(st, o)
            if s < 4:
                z_copy(st, way, s - 1, first, 2).wait_recv()
                if s < 3:
                    z_copy(st, way, s, first, 2).start()
                else:
                    z_copy(st, way, s, first + way, 1).start()
                p_copy(st, o).start()
            else:
                z_copy(st, way, s - 1, first + way, 1).wait_recv()
        if s == 4:
            p_copy(st, 4).start()

    gather_x()
    gather_step(0, 1)
    gather_step(1, 1)
    gather_step(0, 2)

    for i in range(1, NCOL):
        col_copy(i, crel(-i)).wait_recv()

    weight = w[...]
    for b in range(ROW_BLOCKS):
        gagg[b] = lax.dot_general(
            weight, gbuf[b], (((1,), (1,)), ((), ())), preferred_element_type=jnp.float32
        ).astype(jnp.bfloat16)
    for copy in tile_copies:
        copy.wait()

    def tile_step(base, i, acc, product):
        terms = []
        for u in range(UNROLL):
            v = plan[base + i * UNROLL + u]
            terms.append(product((v // 256) % 256, v % 256))
        for u in range(UNROLL):
            k = i * UNROLL + u
            here = plan[base + k] // 65536
            before = plan[base + jnp.maximum(k - 1, 0)] // 65536
            keep = jnp.where(here == before, 1.0, 0.0)
            acc = acc * keep + terms[u]
            runs[k] = acc
        return acc

    def backward(t, o):
        return jnp.dot(gagg[o], tv[t], preferred_element_type=jnp.float32)

    def forward(t, o):
        return jnp.dot(tv[t], fbuf[o], preferred_element_type=jnp.float32)

    def backward_body(i, acc):
        for at, st, s in ((1, 1, 2), (3, 0, 3), (6, 1, 3)):
            @pl.when(i == at)
            def _(st=st, s=s):
                gather_step(st, s)
        return tile_step(B_ORDER, i, acc, backward)

    zero = jnp.zeros((TB, F), jnp.float32)
    lax.fori_loop(0, STEPS, backward_body, zero)

    def extract(which, first, size):
        k = 1 - core if which == 0 else core

        def body(q, carry):
            j = q // 4
            rel = lax.rem(q // 2, 2)
            blk = lax.rem(q, 2)
            o = jnp.where(
                j == 0, 4, jnp.where(j == 7, 0, jnp.where(lax.rem(j, 2) == 1, 3 - j // 2, 4 + j // 2))
            )
            a = jnp.where(rel == 1, xh, 1 - xh)
            b = 2 * rid(a, lax.rem(z + o, NZ), k) + blk
            part[which, j, rel, blk] = runs[plan[B_LAST + b]].astype(jnp.bfloat16)
            return carry

        lax.fori_loop(4 * first, 4 * (first + size), body, 0)

    def peer_copy(n):
        first, size = PIECES[n]
        return remote(
            part.at[0, pl.ds(first, size)], peer.at[pl.ds(first, size)],
            rp_s.at[n], rp_r.at[n], partner,
        )

    for n, (first, size) in enumerate(PIECES):
        extract(0, first, size)
        peer_copy(n).start()
    extract(1, 0, NZ)

    gather_step(0, 4)
    gather_step(1, 4)

    def ring_copy(way, t, rel):
        if t == 0:
            src, dst = ring_out.at[way, t, rel, way], ring_in.at[way, t, rel, way]
        else:
            src, dst = ring_out.at[way, t, rel], ring_in.at[way, t, rel]
        return remote(
            src, dst, rz_s.at[way, t, rel], rz_r.at[way, t, rel], up if way == 0 else down
        )

    def own(j, rel, blk):
        return part[1, j, rel, blk].astype(jnp.float32) + peer[j, rel, blk].astype(jnp.float32)

    def ring_step(t):
        peer_copy(t).wait_recv()
        for rel in range(2):
            for way in range(2):
                j = 0 if t == 0 else 2 * t - 1 + way
                if t > 0:
                    ring_copy(way, t - 1, rel).wait_recv()
                for blk in range(2):
                    if t == 0 and blk != way:
                        continue
                    value = own(j, rel, blk)
                    if t > 1 or (t == 1 and blk == way):
                        value = value + ring_in[way, t - 1, rel, blk].astype(jnp.float32)
                    ring_out[way, t, rel, blk] = value.astype(jnp.bfloat16)
                ring_copy(way, t, rel).start()

    def ring_end(rel):
        total = []
        for way in range(2):
            ring_copy(way, 3, rel).wait_recv()
        for blk in range(2):
            total.append(
                own(7, rel, blk)
                + ring_in[0, 3, rel, blk].astype(jnp.float32)
                + ring_in[1, 3, rel, blk].astype(jnp.float32)
            )
        return total

    ring_step(0)

    for st in range(2):
        for o in range(NZ):
            p_copy(st, o, mine=False).wait_recv()

    def forward_body(i, acc):
        @pl.when(i == 5)
        def _():
            ring_step(1)

        return tile_step(F_ORDER, i, acc, forward)

    lax.fori_loop(0, STEPS, forward_body, zero)

    for b in range(ROW_BLOCKS):
        agg[b] = runs[plan[F_LAST + b]].astype(jnp.bfloat16)

    def agg_copy(i):
        return remote(
            agg.at[pl.ds(2 * crel(i), 2)], agg_in.at[i - 1], cr_s.at[i - 1], cr_r.at[i - 1], cpeer[i]
        )

    for i in range(1, NCOL):
        agg_copy(i).start()

    term = lax.dot_general(
        agg[...].reshape(ROW_BLOCKS * TB, F), gbuf[...].reshape(ROW_BLOCKS * TB, F),
        (((0,), (0,)), ((), ())), preferred_element_type=jnp.float32,
    )
    wt[...] = term.reshape(NCOL, F // NCOL, F)

    def red1_copy(i):
        return remote(wt.at[crel(i)], red1.at[i - 1], a1_s.at[i - 1], a1_r.at[i - 1], cpeer[i])

    quad = xh * 2 + core
    quad_peer = (None, partner, opposite, diagonal)

    def quad_of(i):
        k = core if i % 2 == 0 else 1 - core
        return (xh if i < 2 else 1 - xh) * 2 + k

    def red2_copy(i, owner):
        here = red2.at[owner]
        return remote(here, here, a2_s.at[i - 1], a2_r.at[i - 1], quad_peer[i])

    def red3_copy(i, owner):
        here = red3.at[owner]
        return remote(here, here, a3_s.at[i - 1], a3_r.at[i - 1], zpeer[i])

    def red4_copy(i, owner):
        here = red4.at[owner]
        return remote(here, here, a4_s.at[i - 1], a4_r.at[i - 1], cpeer[i])

    for i in range(1, NCOL):
        red1_copy(i).start()

    ring_step(2)

    for i in range(1, NCOL):
        red1_copy(i).wait_recv()
    total = wt[c]
    for i in range(NCOL - 1):
        total = total + red1[i]
    red2[quad] = total
    for i in range(1, 4):
        red2_copy(i, quad).start()

    for i in range(1, NCOL):
        agg_copy(i).wait_recv()
    for blk in range(2):
        total = agg[2 * c + blk].astype(jnp.float32)
        for i in range(NCOL - 1):
            total = total + agg_in[i, blk].astype(jnp.float32)
        lay_ref[blk] = jnp.dot(
            total.astype(jnp.bfloat16), w[...], preferred_element_type=jnp.float32
        ).astype(jnp.bfloat16)

    ring_step(3)

    for i in range(1, 4):
        red2_copy(i, quad_of(i)).wait_recv()
    red3[z] = red2[0] + red2[1] + red2[2] + red2[3]
    for i in range(1, NZ):
        red3_copy(i, z).start()

    peer_copy(4).wait_recv()
    out = ring_end(0)
    for blk in range(2):
        x_out[blk] = out[blk].astype(jnp.bfloat16)
    last_copy = remote(x_out, x_in, rx.at[0], rx.at[1], opposite)
    last_copy.start()

    for i in range(1, NZ):
        red3_copy(i, zrel(-i)).wait_recv()
    total = red3[0]
    for i in range(1, NZ):
        total = total + red3[i]
    red4[c] = total * (1.0 / math.sqrt(65536))
    for i in range(1, NCOL):
        red4_copy(i, c).start()

    out = ring_end(1)
    last_copy.wait_recv()
    for blk in range(2):
        total = out[blk] + x_in[blk].astype(jnp.float32)
        gf_ref[blk] = total.T.astype(jnp.bfloat16)

    for i in range(1, NCOL):
        red4_copy(i, crel(-i)).wait_recv()
    gw_ref[...] = red4[...].reshape(F, F)

    for i in range(1, NCOL):
        col_copy(i, c).wait_send()
        agg_copy(i).wait_send()
        red1_copy(i).wait_send()
        red3_copy(i, z).wait_send()
        red4_copy(i, c).wait_send()
    for i in range(1, 4):
        red2_copy(i, quad).wait_send()
    x_copy(2 * r).wait_send()
    last_copy.wait_send()
    for n in range(len(PIECES)):
        peer_copy(n).wait_send()
    for st in range(2):
        for o in range(NZ):
            p_copy(st, o).wait_send()
        for way in range(2):
            for step in range(4):
                z_copy(st, way, step, shard(st, 0), 2 if step < 3 else 1).wait_send()
                ring_copy(way, step, st).wait_send()


def per_device(features, tiles, tile_rows, tile_cols, tile_count, weight, grad_out):
    plan = tile_plan(tile_rows[0, 0], tile_cols[0, 0], tile_count[0, 0])
    bf, f32 = jnp.bfloat16, jnp.float32
    dma = pltpu.SemaphoreType.DMA
    vmem = pl.BlockSpec(memory_space=pltpu.VMEM)
    lay, gf, gw = pl.pallas_call(
        kernel,
        out_shape=(
            jax.ShapeDtypeStruct((2, TB, F), bf),
            jax.ShapeDtypeStruct((2, TB, F), bf),
            jax.ShapeDtypeStruct((F, F), f32),
        ),
        in_specs=[
            pl.BlockSpec(memory_space=pltpu.SMEM), vmem, vmem, vmem,
            pl.BlockSpec(memory_space=pl.ANY),
        ],
        out_specs=(vmem, vmem, vmem),
        scratch_shapes=[
            pltpu.VMEM((SLOTS, TB, TB), bf),
            pltpu.VMEM((COL_BLOCKS, TB, F), bf),
            pltpu.VMEM((ROW_BLOCKS, TB, F), bf),
            pltpu.VMEM((ROW_BLOCKS, F, TB), bf),
            pltpu.VMEM((SLOTS + 1, TB, F), f32),
            pltpu.VMEM((2, NZ, 2, 2, F, TB), bf),
            pltpu.VMEM((NZ, 2, 2, F, TB), bf),
            pltpu.VMEM((2, 4, 2, 2, F, TB), bf),
            pltpu.VMEM((2, 4, 2, 2, F, TB), bf),
            pltpu.VMEM((2, F, TB), bf),
            pltpu.VMEM((2, F, TB), bf),
            pltpu.VMEM((ROW_BLOCKS, TB, F), bf),
            pltpu.VMEM((NCOL - 1, 2, TB, F), bf),
            pltpu.VMEM((NCOL, F // NCOL, F), f32),
            pltpu.VMEM((NCOL - 1, F // NCOL, F), f32),
            pltpu.VMEM((4, F // NCOL, F), f32),
            pltpu.VMEM((NZ, F // NCOL, F), f32),
            pltpu.VMEM((NCOL, F // NCOL, F), f32),
            dma((4,)), dma((7,)), dma((7,)), dma((2, 2, 4)), dma((2, 2, 4)), dma((2,)),
            dma((2, NZ)), dma((2, NZ)), dma((5,)), dma((5,)), dma((2, 4, 2)), dma((2, 4, 2)),
            dma((2,)), dma((7,)), dma((7,)), dma((7,)), dma((7,)), dma((3,)), dma((3,)),
            dma((7,)), dma((7,)), dma((7,)), dma((7,)),
        ],
        compiler_params=pltpu.CompilerParams(
            collective_id=0, has_side_effects=True, vmem_limit_bytes=48 * 2**20
        ),
        cost_estimate=pl.CostEstimate(flops=2 * 2 * SLOTS * TB * TB * F, bytes_accessed=2**23, transcendentals=0),
        name="aggregate",
    )(
        plan,
        features.reshape(2, TB, F),
        grad_out.reshape(2, TB, F),
        weight,
        tiles.reshape(SLOTS, TB, TB),
    )
    return (lay.reshape(1, 2 * TB, F), gf.reshape(1, 2 * TB, F), gw)


def solution(mesh):
    in_specs = (
        P("col", "row", None),
        P("row", "col", None, None, None),
        P("row", "col", None),
        P("row", "col", None),
        P("row", "col"),
        P(),
        P("row", "col", None),
    )
    out_specs = (P("row", "col", None), P("col", "row", None), P())
    return jax.shard_map(
        per_device, mesh=mesh, in_specs=in_specs, out_specs=out_specs, check_vma=False
    )
```

time: 556 us -> 74.7 us (0.13)
  waiting for transfers between devices: 386 us -> 0 us
  Pallas kernels: 0 us -> 65.2 us
  local copies, waits for them, and re-layouts: 57.8 us -> 4.34 us
  matrix products: 48.2 us -> 0 us
  blocking collectives: 26.1 us -> 0 us
  other arithmetic: 18.4 us -> 2.84 us
  between operations: 14.5 us -> 1.34 us
    psum x1 -> x0, waiting for transfers between devices: 236 us -> none  [per_device(): grad_weight = lax.psum(weight_term, ('row', 'col')) / math.sqrt(node_total)]
    reduce_scatter x2 -> x0, waiting for transfers between devices: 132 us -> none  [the longest x1 114 us: per_device(): lax.psum_scatter(back_partial.astype(jnp.bfloat16), 'row', scatter_dimens...]
    pallas_call x0 -> x1, Pallas kernels: none -> 65.2 us  [per_device(): pl.pallas_call(kernel, out_shape=(jax.ShapeDtypeStruct((2, TB, F), bf), j...]
    dot_general x9 -> x0, matrix products: 48.2 us -> none  [the longest x2 28.4 us: slot_products(): jnp.einsum(pattern, tile_slots, picked, preferred_element_type=jnp.float32)]
    mul x2 -> x0, local copies, waits for them, and re-layouts: 35.6 us -> none  [slot_products(): product = product * live_mask.astype(jnp.float32)[:, None, None]]
    all_gather x1 -> x0, blocking collectives: 26.1 us -> none  [per_device(): row_group = lax.all_gather(grad_agg, 'col', axis=0, tiled=True)]
    gather x2 -> x0, local copies, waits for them, and re-layouts: 18.8 us -> none  [the longest x1 10.2 us: per_device(): picked = column_blocks[slot_cols]]
    all_gather x1 -> x0, waiting for transfers between devices: 16.8 us -> none  [per_device(): column_group = lax.all_gather(features, 'row', axis=1, tiled=True)[0]]
  transfers between devices with their start and end apart: 4 -> 0, of which waited for: 4 -> 0; matrix products, arithmetic and copies ran while one was open for 13% -> 0% of each run, Pallas kernels for 0% -> 0%
where the time goes in v1:
time: 74.7 us; the launch traced here: 73.7 us
  Pallas kernels  65.2 us (87%)
  local copies, waits for them, and re-layouts  4.34 us (6%)
  other arithmetic  2.84 us (4%)
  between operations  1.34 us (2%)
    pallas_call x1, Pallas kernels, per_device(): pl.pallas_call(kernel, out_shape=(jax.ShapeDtypeStruct((2, TB, F), bf), j...  65.2 us
    unnamed x9, local copies, waits for them, and re-layouts  4.33 us

profile of v1, /device:TPU:1, one launch (start us, length us, event | category | flops | bytes accessed | tf_op | source)
XLA Modules:
  0.0 73.7 jit_solution(732156254534725638)
XLA Ops:
  1.3 0.7 compare_select_fusion
  2.0 0.7 fusion.3
  2.7 0.7 fusion.2
  3.4 0.2 convert_reduce_fusion
  3.7 0.2 select_reduce_fusion
  3.8 0.1 fusion
  3.9 0.1 convert_reduce_fusion.1
  4.1 0.1 pad_add_fusion.plan
  4.2 0.0 copy-start
  4.2 0.8 %copy-done = bf16[1,256,128]{2,1,0:T(8,128)(2,1)S(1)} copy-done((bf16[1,256,128]{2,1,0:T(8,128)(2,1)S(1)}, bf16[1,256,128]{2,1,0:T(8,128)(2,1)}, u32[]{:S(2)}) %copy-start) | copy-done | bytes 65560
  5.0 0.0 copy-start.1
  5.0 0.8 %copy-done.1 = bf16[1,256,128]{2,1,0:T(8,128)(2,1)S(1)} copy-done((bf16[1,256,128]{2,1,0:T(8,128)(2,1)S(1)}, bf16[1,256,128]{2,1,0:T(8,128)(2,1)}, u32[]{:S(2)}) %copy-start.1) | copy-done | bytes 65560
  5.9 0.0 copy-start.2
  5.9 0.8 %copy-done.2 = bf16[128,128]{1,0:T(8,128)(2,1)S(1)} copy-done((bf16[128,128]{1,0:T(8,128)(2,1)S(1)}, bf16[128,128]{1,0:T(8,128)(2,1)}, u32[]{:S(2)}) %copy-start.2) | copy-done | bytes 32792
  6.6 65.2 %aggregate.1 = (bf16[2,128,128]{2,1,0:T(8,128)(2,1)S(1)}, bf16[2,128,128]{2,1,0:T(8,128)(2,1)S(1)}, f32[128,128]{1,0:T(8,128)S(1)}) custom-call(s32[592]{0:T(1024)S(1)} %pad_add_fusion.plan, bf16[2,128,128]{2,1,0:T(8,128)(2,1)S(1)} %bitcast.22, bf16[2,128,128]{2,1,0:T(8,128)(2,1)S(1)} %bitcast.23, bf16[128,128]{1,0:T(8,128)(2,1)S(1)} %copy-done.2, ...), custom_call_target="tpu_custom_call" | custom-call | flops 2147483648 | bytes 8388608 | tf_op jit(solution)/shard_map/aggregate/pallas_call | solution.py:409
  71.8 0.6 copy.14
  72.5 0.6 copy.15
  73.1 0.6 copy.16
  (5 shorter events, 0.0 us)
Async XLA Ops:
  4.2 0.8 %copy-start = (bf16[1,256,128]{2,1,0:T(8,128)(2,1)S(1)}, bf16[1,256,128]{2,1,0:T(8,128)(2,1)}, u32[]{:S(2)}) copy-start(bf16[1,256,128]{2,1,0:T(8,128)(2,1)} %param.7) | copy-start | bytes 196612
  5.0 0.8 %copy-start.1 = (bf16[1,256,128]{2,1,0:T(8,128)(2,1)S(1)}, bf16[1,256,128]{2,1,0:T(8,128)(2,1)}, u32[]{:S(2)}) copy-start(bf16[1,256,128]{2,1,0:T(8,128)(2,1)} %param.13) | copy-start | bytes 196612
  5.9 0.8 %copy-start.2 = (bf16[128,128]{1,0:T(8,128)(2,1)S(1)}, bf16[128,128]{1,0:T(8,128)(2,1)}, u32[]{:S(2)}) copy-start(bf16[128,128]{1,0:T(8,128)(2,1)} %w.1) | copy-start | bytes 98308

commit v2 on v0

v2 whole, which is shorter than its diff:
```python
import math

import jax
import jax.numpy as jnp
from jax import lax
from jax.experimental import pallas as pl
from jax.experimental.pallas import tpu as pltpu
from jax.sharding import PartitionSpec as P

TB = 128
F = 128
SLOTS = 256
ROW_BLOCKS = 16
COL_BLOCKS = 64
NZ = 8
NCOL = 8
UNROLL = 32
STEPS = SLOTS // UNROLL
EMPTY = SLOTS
KEY_BITS = 16
SLOT_BITS = 8
OFFSETS = (4, 3, 5, 2, 6, 1, 7, 0)
PIECES = ((0, 1), (1, 2), (3, 2), (5, 3))
NEXT, SECOND, THIRD, FOURTH, NEXT_B = range(5)
B_ORDER, B_LAST, F_ORDER, F_LAST = range(4)


def remote(src, dst, send, recv, device):
    return pltpu.make_async_remote_copy(
        src_ref=src, dst_ref=dst, send_sem=send, recv_sem=recv,
        device_id=device, device_id_type=pl.DeviceIdType.MESH,
    )


def sorted_plan(key, other, count):
    lane = lax.broadcasted_iota(jnp.int32, (1, SLOTS), 1)
    key = jnp.where(lane < count, key, COL_BLOCKS)
    value = (key * 2**KEY_BITS + lane * 2**SLOT_BITS + other).astype(jnp.float32)
    across = lax.broadcasted_iota(jnp.int32, (SLOTS, SLOTS), 1)
    along = lax.broadcasted_iota(jnp.int32, (SLOTS, SLOTS), 0)
    column = jnp.sum(jnp.where(across == along, value, 0.0), axis=1, keepdims=True)
    place = jnp.sum(jnp.where(value < column, 1.0, 0.0), axis=1, keepdims=True)
    order = jnp.sum(jnp.where(place == across.astype(jnp.float32), column, 0.0), axis=0, keepdims=True)
    bound = (lane * 2**KEY_BITS).astype(jnp.float32)
    below = jnp.sum(jnp.where(column < bound, 1.0, 0.0), axis=0, keepdims=True)
    upto = jnp.sum(jnp.where(column < bound + 2.0**KEY_BITS, 1.0, 0.0), axis=0, keepdims=True)
    last = jnp.where(upto > below, upto - 1.0, float(EMPTY))
    return order.astype(jnp.int32), last.astype(jnp.int32)


def kernel(
    count, rows_hbm, cols_hbm, feat_hbm, gout_hbm, w_hbm, tiles_hbm, lay_ref, gf_ref, gw_ref,
    rows, cols, gin, w, plan_v, plan,
    tv, fbuf, gbuf, runs, part, peer, x_out, x_in, z_out, z_in,
    agg, agg_in, wt, red1, red2, red3, red4,
    load, tile_sem, plan_sem, col_s, col_r, agz_s, agz_r, agx_s, agx_r, agp_s, agp_r,
    rp_s, rp_r, rx_s, rx_r, rz_s, rz_r, cr_s, cr_r,
    a1_s, a1_r, a2_s, a2_r, a3_s, a3_r, a4_s, a4_r,
):
    r = lax.axis_index("row")
    c = lax.axis_index("col")
    core = lax.rem(r, 2)
    z = lax.rem(r // 2, NZ)
    xh = r // (2 * NZ)

    def rid(a, b, k):
        return (a * NZ + b) * 2 + k

    def zrel(o):
        return lax.rem(z + (o % NZ), NZ)

    def crel(o):
        return lax.rem(c + (o % NCOL), NCOL)

    def cid(yo, near):
        side = lax.rem(c, 2)
        return 2 * lax.rem(c // 2 + (yo % 4), 4) + (side if near == 0 else 1 - side)

    partner = (rid(xh, z, 1 - core), c)
    opposite = (rid(1 - xh, z, core), c)
    diagonal = (rid(1 - xh, z, 1 - core), c)
    beside = (r, cid(0, 1))
    ypeer = [None] + [(r, cid(i, 0)) for i in range(1, 4)]
    zpeer = [None] + [(rid(xh, zrel(i), core), c) for i in range(1, NZ)]
    cpeer = [None] + [(r, crel(i)) for i in range(1, NCOL)]
    far_first = (4, 3, 5, 2, 6, 1, 7)

    loads = [
        pltpu.make_async_copy(src, dst, load.at[i])
        for i, (src, dst) in enumerate(
            (
                (gout_hbm, gin),
                (feat_hbm, fbuf.at[pl.ds(2 * r, 2)]),
                (rows_hbm, rows),
                (cols_hbm, cols),
                (w_hbm, w),
            )
        )
    ]
    tile_copies = [
        pltpu.make_async_copy(
            tiles_hbm.at[pl.ds(64 * i, 64)], tv.at[pl.ds(64 * i, 64)], tile_sem.at[i]
        )
        for i in range(4)
    ]
    for copy in loads:
        copy.start()
    for copy in tile_copies:
        copy.start()
    barrier = pltpu.get_barrier_semaphore()
    everyone = zpeer[1:] + cpeer[1:] + [partner, opposite, diagonal]
    for device in everyone:
        pl.semaphore_signal(
            barrier, inc=1, device_id=device, device_id_type=pl.DeviceIdType.MESH
        )
    runs[EMPTY] = jnp.zeros((TB, F), jnp.float32)
    loads[0].wait()
    for blk in range(2):
        gbuf[2 * c + blk] = gin[blk].astype(jnp.float32).T.astype(jnp.bfloat16)
    loads[1].wait()
    pl.semaphore_wait(barrier, len(everyone))

    def col_shard(yo, near):
        return gbuf.at[pl.ds(2 * cid(yo, near), 2)]

    def col_copy(i, near, yo):
        here = col_shard(yo, near)
        return remote(here, here, col_s.at[near, i], col_r.at[near, i], ypeer[i])

    def side_copy(near):
        here = col_shard(0, near)
        return remote(here, here, col_s.at[0, 0], col_r.at[0, 0], beside)

    def shard(st, o, k):
        return fbuf.at[pl.ds(2 * rid(xh if st == 0 else 1 - xh, zrel(o), k), 2)]

    def z_copy(kind, way, o):
        sign = 1 if way == 0 else -1
        here = shard(1 if kind == NEXT_B else 0, o, core)
        if kind == FOURTH:
            here = fbuf.at[pl.ds(2 * rid(xh, zrel(o), core) + way, 1)]
        step = 2 if kind in (SECOND, FOURTH) else 1
        return remote(
            here, here, agz_s.at[kind, way], agz_r.at[kind, way], zpeer[(sign * step) % NZ]
        )

    def x_copy(o, st):
        here = shard(st, o, core)
        return remote(here, here, agx_s.at[o % NZ], agx_r.at[o % NZ], opposite)

    def p_copy(st, o, k):
        here = shard(st, o, k)
        return remote(here, here, agp_s.at[st, o % NZ], agp_r.at[st, o % NZ], partner)

    side_copy(0).start()
    for i in (2, 1, 3):
        col_copy(i, 0, 0).start()
    x_copy(0, 0).start()
    for kind in (SECOND, NEXT):
        for way in range(2):
            z_copy(kind, way, 0).start()
    p_copy(0, 0, core).start()

    def arrive_z(kind, way):
        back = (1, 2, 3, 4, 1)[kind]
        o = -back if way == 0 else back
        z_copy(kind, way, o).wait_recv()
        if kind == SECOND:
            z_copy(THIRD, way, o).start()
            z_copy(FOURTH, way, o).start()
        if kind in (SECOND, THIRD):
            x_copy(o, 0).start()
        if kind == FOURTH:
            if way == 0:
                return
            x_copy(4, 0).start()
        p_copy(1 if kind == NEXT_B else 0, o, core).start()

    def arrive_x(o):
        x_copy(o, 1).wait_recv()
        if o == 0:
            for way in range(2):
                z_copy(NEXT_B, way, 0).start()
        p_copy(1, o, core).start()

    def arrive_side():
        side_copy(1).wait_recv()
        for i in (2, 1, 3):
            col_copy(i, 1, 0).start()

    arrive_side()
    arrive_x(0)
    for way in range(2):
        arrive_z(NEXT, way)

    loads[2].wait()
    loads[3].wait()
    live = count[0, 0]
    order, last = sorted_plan(cols[...], rows[...], live)
    plan_v[pl.ds(B_ORDER, 1)] = order
    plan_v[pl.ds(B_LAST, 1)] = last
    order, last = sorted_plan(rows[...], cols[...], live)
    plan_v[pl.ds(F_ORDER, 1)] = order
    plan_v[pl.ds(F_LAST, 1)] = last
    plan_copy = pltpu.make_async_copy(plan_v, plan, plan_sem.at[0])
    plan_copy.start()

    for way in range(2):
        arrive_z(SECOND, way)

    plan_copy.wait()
    for copy in tile_copies:
        copy.wait()
    loads[4].wait()
    for near in range(2):
        for i in range(1, 4):
            col_copy(i, near, -i).wait_recv()

    def tile_step(which, i, acc, product):
        value = [plan[which, i * UNROLL + u] for u in range(UNROLL)]
        before = [plan[which, jnp.maximum(i * UNROLL - 1, 0)]] + value[:-1]
        terms = []
        for v in value:
            terms.append(product((v >> SLOT_BITS) & (SLOTS - 1), v))
        for u in range(UNROLL):
            same = (value[u] >> KEY_BITS) == (before[u] >> KEY_BITS)
            acc = acc * jnp.where(same, 1.0, 0.0) + terms[u]
            runs[i * UNROLL + u] = acc
        return acc

    def final_run(which, block):
        last = jnp.clip(plan[which, block], 0, EMPTY)
        return runs[last].astype(jnp.bfloat16)

    def backward(t, o):
        return jnp.dot(gbuf[o & (ROW_BLOCKS - 1)], tv[t], preferred_element_type=jnp.float32)

    def forward(t, o):
        return jnp.dot(tv[t], fbuf[o & (COL_BLOCKS - 1)], preferred_element_type=jnp.float32)

    def backward_body(i, acc):
        @pl.when(i == 0)
        def _():
            for way in range(2):
                arrive_z(THIRD, way)

        @pl.when(i == 2)
        def _():
            for way in range(2):
                arrive_z(FOURTH, way)
                arrive_z(NEXT_B, way)

        @pl.when(i == 5)
        def _():
            arrive_x(2)
            arrive_x(6)

        return tile_step(B_ORDER, i, acc, backward)

    zero = jnp.zeros((TB, F), jnp.float32)
    lax.fori_loop(0, STEPS, backward_body, zero)

    def block_of(which, j, rel):
        k = 1 - core if which == 0 else core
        o = jnp.where(
            j == 0, 4, jnp.where(j == 7, 0, jnp.where(lax.rem(j, 2) == 1, 3 - j // 2, 4 + j // 2))
        )
        a = jnp.where(rel == 1, xh, 1 - xh)
        return 2 * rid(a, lax.rem(z + o, NZ), k)

    def extract(which, first, size):
        def body(q, carry):
            j = q // 2
            rel = lax.rem(q, 2)
            b = block_of(which, j, rel)
            for blk in range(2):
                part[which, j, rel, blk] = final_run(B_LAST, b + blk)
            return carry

        lax.fori_loop(2 * first, 2 * (first + size), body, 0)

    def peer_copy(n):
        first, size = PIECES[n]
        return remote(
            part.at[0, pl.ds(first, size)], peer.at[pl.ds(first, size)],
            rp_s.at[n], rp_r.at[n], partner,
        )

    def rx_copy(o):
        return remote(x_out.at[o], x_in.at[o], rx_s.at[o], rx_r.at[o], opposite)

    def rz_copy(kind, way):
        sign = 1 if way == 0 else -1
        src, dst = z_out.at[kind, way], z_in.at[kind, way]
        if kind == FOURTH:
            src, dst = z_out.at[kind, way, way], z_in.at[kind, way, way]
        step = 2 if kind in (SECOND, FOURTH) else 1
        return remote(src, dst, rz_s.at[kind, way], rz_r.at[kind, way], zpeer[(sign * step) % NZ])

    def own(j, rel, blk):
        return part[1, j, rel, blk].astype(jnp.float32) + peer[j, rel, blk].astype(jnp.float32)

    for n, (first, size) in enumerate(PIECES):
        extract(0, first, size)
        peer_copy(n).start()
    extract(1, 0, NZ)
    place = {o: j for j, o in enumerate(OFFSETS)}

    def send_x(o):
        for blk in range(2):
            value = own(place[o], 0, blk)
            if o == 0:
                for way in range(2):
                    value = value + z_in[NEXT_B, way, blk].astype(jnp.float32)
            x_out[o, blk] = value.astype(jnp.bfloat16)
        rx_copy(o).start()

    def send_z(kind, way):
        o = (1, 2, 3, 4, 1)[kind] * (1 if way == 0 else -1) % NZ
        rel = 0 if kind == NEXT_B else 1
        if kind in (SECOND, THIRD) or (kind == FOURTH and way == 0):
            rx_copy(o).wait_recv()
        if kind == SECOND:
            for other in (THIRD, FOURTH):
                rz_copy(other, way).wait_recv()
        for blk in range(2):
            if kind == FOURTH and blk != way:
                continue
            value = own(place[o], rel, blk)
            if kind in (SECOND, THIRD, FOURTH):
                value = value + x_in[o, blk].astype(jnp.float32)
            if kind == SECOND:
                value = value + z_in[THIRD, way, blk].astype(jnp.float32)
                if blk == way:
                    value = value + z_in[FOURTH, way, blk].astype(jnp.float32)
            z_out[kind, way, blk] = value.astype(jnp.bfloat16)
        rz_copy(kind, way).start()

    for n in range(len(PIECES)):
        peer_copy(n).wait_recv()
        for o in ((4,), (3, 5), (2, 6), ())[n]:
            send_x(o)
    for kind in (NEXT_B, NEXT):
        for way in range(2):
            send_z(kind, way)

    for o in (3, 5, 4):
        arrive_x(o)
    for st in range(2):
        for o in range(NZ):
            p_copy(st, o, 1 - core).wait_recv()

    def term_body(j, acc):
        for which in range(2):
            for rel in range(2):
                b = block_of(which, j, rel)
                left = jnp.concatenate([part[which, j, rel, 0], part[which, j, rel, 1]], axis=1)
                right = fbuf[pl.ds(b, 2)].reshape(2 * TB, F)
                acc = acc + jnp.dot(left, right, preferred_element_type=jnp.float32)
        return acc

    term = lax.fori_loop(0, NZ, term_body, zero)
    wt[...] = term.reshape(NCOL, F // NCOL, F)

    def red1_copy(i):
        return remote(wt.at[crel(i)], red1.at[i - 1], a1_s.at[i - 1], a1_r.at[i - 1], cpeer[i])

    quad = xh * 2 + core
    quad_peer = (None, partner, opposite, diagonal)

    def quad_of(i):
        k = core if i % 2 == 0 else 1 - core
        return (xh if i < 2 else 1 - xh) * 2 + k

    def red2_copy(i, owner):
        here = red2.at[owner]
        return remote(here, here, a2_s.at[i - 1], a2_r.at[i - 1], quad_peer[i])

    def red3_copy(i, owner):
        here = red3.at[owner]
        return remote(here, here, a3_s.at[i - 1], a3_r.at[i - 1], zpeer[i])

    def red4_copy(i, owner):
        here = red4.at[owner]
        return remote(here, here, a4_s.at[i - 1], a4_r.at[i - 1], cpeer[i])

    for i in (5, 3, 4, 6, 2, 7, 1):
        red1_copy(i).start()

    lax.fori_loop(0, STEPS, lambda i, acc: tile_step(F_ORDER, i, acc, forward), zero)

    for b in range(ROW_BLOCKS):
        agg[b] = final_run(F_LAST, b)

    def agg_copy(i):
        return remote(
            agg.at[pl.ds(2 * crel(i), 2)], agg_in.at[i - 1], cr_s.at[i - 1], cr_r.at[i - 1], cpeer[i]
        )

    for i in (5, 3, 4, 6, 2, 7, 1):
        agg_copy(i).start()

    for way in range(2):
        send_z(FOURTH, way)
    for way in range(2):
        send_z(THIRD, way)
    for way in range(2):
        rz_copy(NEXT_B, way).wait_recv()
    send_x(0)

    for i in range(1, NCOL):
        red1_copy(i).wait_recv()
    total = wt[c]
    for i in range(NCOL - 1):
        total = total + red1[i]
    red2[quad] = total
    for i in (3, 2, 1):
        red2_copy(i, quad).start()

    for i in range(1, 4):
        red2_copy(i, quad_of(i)).wait_recv()
    red3[z] = red2[0] + red2[1] + red2[2] + red2[3]
    for i in far_first:
        red3_copy(i, z).start()

    for way in range(2):
        send_z(SECOND, way)

    for i in range(1, NCOL):
        agg_copy(i).wait_recv()
    for blk in range(2):
        total = agg[2 * c + blk].astype(jnp.float32)
        for i in range(NCOL - 1):
            total = total + agg_in[i, blk].astype(jnp.float32)
        lay_ref[blk] = jnp.dot(
            total.astype(jnp.bfloat16), w[...], preferred_element_type=jnp.float32
        ).astype(jnp.bfloat16)

    for i in range(1, NZ):
        red3_copy(i, zrel(-i)).wait_recv()
    total = red3[0]
    for i in range(1, NZ):
        total = total + red3[i]
    red4[c] = total * (1.0 / math.sqrt(65536))
    for i in (5, 3, 4, 6, 2, 7, 1):
        red4_copy(i, c).start()

    rx_copy(0).wait_recv()
    for kind in (NEXT, SECOND):
        for way in range(2):
            rz_copy(kind, way).wait_recv()
    for blk in range(2):
        total = own(place[0], 1, blk) + x_in[0, blk].astype(jnp.float32)
        for kind in (NEXT, SECOND):
            for way in range(2):
                total = total + z_in[kind, way, blk].astype(jnp.float32)
        upper = total.astype(jnp.bfloat16)
        lower = (total - upper.astype(jnp.float32)).astype(jnp.bfloat16)
        value = jnp.zeros((TB, F), jnp.float32)
        for share in (lower, upper):
            value = value + lax.dot_general(
                share, w[...], (((0,), (1,)), ((), ())), preferred_element_type=jnp.float32
            )
        gf_ref[blk] = value.astype(jnp.bfloat16)

    for i in range(1, NCOL):
        red4_copy(i, crel(-i)).wait_recv()
    gw_ref[...] = red4[...].reshape(F, F).T

    side_copy(0).wait_send()
    for i in range(1, NCOL):
        agg_copy(i).wait_send()
        red1_copy(i).wait_send()
        red3_copy(i, z).wait_send()
        red4_copy(i, c).wait_send()
    for near in range(2):
        for i in range(1, 4):
            col_copy(i, near, 0).wait_send()
    for i in range(1, 4):
        red2_copy(i, quad).wait_send()
    for n in range(len(PIECES)):
        peer_copy(n).wait_send()
    for kind in range(5):
        for way in range(2):
            z_copy(kind, way, 0).wait_send()
            rz_copy(kind, way).wait_send()
    for o in (0, 2, 3, 4, 5, 6):
        x_copy(o, 0).wait_send()
        rx_copy(o).wait_send()
    for st in range(2):
        for o in range(NZ):
            p_copy(st, o, core).wait_send()


def per_device(features, tiles, tile_rows, tile_cols, tile_count, weight, grad_out):
    bf, f32, i32 = jnp.bfloat16, jnp.float32, jnp.int32
    dma = pltpu.SemaphoreType.DMA
    vmem = pl.BlockSpec(memory_space=pltpu.VMEM)
    anywhere = pl.BlockSpec(memory_space=pl.ANY)
    pair = (2, TB, F)
    out_shape = (
        jax.ShapeDtypeStruct(pair, bf),
        jax.ShapeDtypeStruct(pair, bf),
        jax.ShapeDtypeStruct((F, F), f32),
    )
    lay, gf, gw = pl.pallas_call(
        kernel,
        out_shape=out_shape,
        in_specs=[pl.BlockSpec(memory_space=pltpu.SMEM)] + [anywhere] * 6,
        out_specs=(vmem, vmem, vmem),
        scratch_shapes=[
            pltpu.VMEM((1, SLOTS), i32),
            pltpu.VMEM((1, SLOTS), i32),
            pltpu.VMEM(pair, bf),
            pltpu.VMEM((F, F), bf),
            pltpu.VMEM((4, SLOTS), i32),
            pltpu.SMEM((4, SLOTS), i32),
            pltpu.VMEM((SLOTS, TB, TB), bf),
            pltpu.VMEM((COL_BLOCKS, TB, F), bf),
            pltpu.VMEM((ROW_BLOCKS, F, TB), bf),
            pltpu.VMEM((SLOTS + 1, TB, F), f32),
            pltpu.VMEM((2, NZ, 2, 2, F, TB), bf),
            pltpu.VMEM((NZ, 2, 2, F, TB), bf),
            pltpu.VMEM((NZ, 2, F, TB), bf),
            pltpu.VMEM((NZ, 2, F, TB), bf),
            pltpu.VMEM((5, 2, 2, F, TB), bf),
            pltpu.VMEM((5, 2, 2, F, TB), bf),
            pltpu.VMEM((ROW_BLOCKS, TB, F), bf),
            pltpu.VMEM((NCOL - 1, 2, TB, F), bf),
            pltpu.VMEM((NCOL, F // NCOL, F), f32),
            pltpu.VMEM((NCOL - 1, F // NCOL, F), f32),
            pltpu.VMEM((4, F // NCOL, F), f32),
            pltpu.VMEM((NZ, F // NCOL, F), f32),
            pltpu.VMEM((NCOL, F // NCOL, F), f32),
            dma((5,)), dma((4,)), dma((1,)), dma((2, 4)), dma((2, 4)), dma((5, 2)), dma((5, 2)),
            dma((NZ,)), dma((NZ,)), dma((2, NZ)), dma((2, NZ)),
            dma((4,)), dma((4,)), dma((NZ,)), dma((NZ,)), dma((5, 2)), dma((5, 2)), dma((7,)), dma((7,)),
            dma((7,)), dma((7,)), dma((3,)), dma((3,)), dma((7,)), dma((7,)), dma((7,)), dma((7,)),
        ],
        compiler_params=pltpu.CompilerParams(
            collective_id=0, has_side_effects=True, vmem_limit_bytes=63 * 2**20
        ),
        cost_estimate=pl.CostEstimate(
            flops=4 * SLOTS * TB * TB * F, bytes_accessed=2**23, transcendentals=0
        ),
        name="aggregate",
    )(
        tile_count,
        tile_rows.reshape(1, SLOTS),
        tile_cols.reshape(1, SLOTS),
        features.reshape(pair),
        grad_out.reshape(pair),
        weight,
        tiles.reshape(SLOTS, TB, TB),
    )
    return (lay.reshape(1, 2 * TB, F), gf.reshape(1, 2 * TB, F), gw)


def solution(mesh):
    in_specs = (
        P("col", "row", None),
        P("row", "col", None, None, None),
        P("row", "col", None),
        P("row", "col", None),
        P("row", "col"),
        P(),
        P("row", "col", None),
    )
    out_specs = (P("row", "col", None), P("col", "row", None), P())
    return jax.shard_map(
        per_device, mesh=mesh, in_specs=in_specs, out_specs=out_specs, check_vma=False
    )
```

time: 556 us -> 61.9 us (0.11)
  the two profiles are of different devices: /device:TPU:1 before, /device:TPU:2 now
where the time goes in v2:
time: 61.9 us; the launch traced here: 61.7 us
  Pallas kernels  56 us (90%)
  local copies, waits for them, and re-layouts  4.42 us (7%)
  between operations  1.29 us (2%)
    pallas_call x1, Pallas kernels, per_device(): pl.pallas_call(kernel, out_shape=out_shape, in_specs=[pl.BlockSpec(memory...  56 us
    unnamed x3, local copies, waits for them, and re-layouts  4.42 us

profile of v2, /device:TPU:2, one launch (start us, length us, event | category | flops | bytes accessed | tf_op | source)
XLA Modules:
  0.0 61.7 jit_solution(6672331118975858575)
XLA Ops:
  1.3 56.0 %aggregate.1 = (bf16[2,128,128]{2,1,0:T(8,128)(2,1)}, bf16[2,128,128]{2,1,0:T(8,128)(2,1)}, f32[128,128]{1,0:T(8,128)}) custom-call(s32[1,1]{1,0:T(1,128)S(6)} %copy.13.count, s32[1,256]{1,0:T(1,128)} %bitcast.12, s32[1,256]{1,0:T(1,128)} %bitcast.13, bf16[2,128,128]{2,1,0:T(8,128)(2,1)} %bitcast.8, bf16[2,128,128]{2,1,0:T(8,128)(2,1)} %bitcast.9, ...), custom_call_target="tpu_custom_call" | custom-call | flops 2147483648 | bytes 8388608 | tf_op jit(solution)/shard_map/aggregate/pallas_call | solution.py:506
  57.3 1.5 %copy.14 = bf16[1,256,128]{2,1,0:T(8,128)(2,1)} copy(bf16[1,256,128]{2,1,0:T(8,128)(2,1)} %bitcast.11) | data formatting | bytes 131072
  58.8 1.5 %copy.15 = bf16[1,256,128]{2,1,0:T(8,128)(2,1)} copy(bf16[1,256,128]{2,1,0:T(8,128)(2,1)} %bitcast.10) | data formatting | bytes 131072
  60.2 1.5 %copy.16 = f32[128,128]{1,0:T(8,128)} copy(f32[128,128]{1,0:T(8,128)} %get-tuple-element.14) | data formatting | bytes 131072

commit v3 on v2

--- a/solution.py
+++ b/solution.py
@@ -52,10 +52,10 @@
     count, rows_hbm, cols_hbm, feat_hbm, gout_hbm, w_hbm, tiles_hbm, lay_ref, gf_ref, gw_ref,
     rows, cols, gin, w, plan_v, plan,
     tv, fbuf, gbuf, runs, part, peer, x_out, x_in, z_out, z_in,
-    agg, agg_in, wt, red1, red2, red3, red4,
+    agg, agg_in, wt, red1, red2, red3,
     load, tile_sem, plan_sem, col_s, col_r, agz_s, agz_r, agx_s, agx_r, agp_s, agp_r,
     rp_s, rp_r, rx_s, rx_r, rz_s, rz_r, cr_s, cr_r,
-    a1_s, a1_r, a2_s, a2_r, a3_s, a3_r, a4_s, a4_r,
+    a1_s, a1_r, a2_s, a2_r, a3_s, a3_r,
 ):
     r = lax.axis_index("row")
     c = lax.axis_index("col")
@@ -78,12 +78,17 @@
 
     partner = (rid(xh, z, 1 - core), c)
     opposite = (rid(1 - xh, z, core), c)
-    diagonal = (rid(1 - xh, z, 1 - core), c)
     beside = (r, cid(0, 1))
     ypeer = [None] + [(r, cid(i, 0)) for i in range(1, 4)]
+    far = (10, 11, 8, 9, 6, 7, 12, 13, 5, 4, 14, 15, 3, 2, 1)
+
+    def flip(value, i):
+        return value if i % 2 == 0 else 1 - value
+
+    near_peer = [(rid(xh, z, flip(core, i)), crel(i // 2)) for i in range(16)]
+    row_peer = [(rid(flip(xh, i), zrel(i // 2), core), c) for i in range(16)]
     zpeer = [None] + [(rid(xh, zrel(i), core), c) for i in range(1, NZ)]
     cpeer = [None] + [(r, crel(i)) for i in range(1, NCOL)]
-    far_first = (4, 3, 5, 2, 6, 1, 7)
 
     loads = [
         pltpu.make_async_copy(src, dst, load.at[i])
@@ -103,16 +108,16 @@
         )
         for i in range(4)
     ]
+    barrier = pltpu.get_barrier_semaphore()
+    everyone = [zpeer[i] for i in (1, 2, 6, 7)] + ypeer[1:] + [beside, opposite, partner]
+    for device in everyone:
+        pl.semaphore_signal(
+            barrier, inc=1, device_id=device, device_id_type=pl.DeviceIdType.MESH
+        )
     for copy in loads:
         copy.start()
     for copy in tile_copies:
         copy.start()
-    barrier = pltpu.get_barrier_semaphore()
-    everyone = zpeer[1:] + cpeer[1:] + [partner, opposite, diagonal]
-    for device in everyone:
-        pl.semaphore_signal(
-            barrier, inc=1, device_id=device, device_id_type=pl.DeviceIdType.MESH
-        )
     runs[EMPTY] = jnp.zeros((TB, F), jnp.float32)
     loads[0].wait()
     for blk in range(2):
@@ -156,9 +161,8 @@
     for i in (2, 1, 3):
         col_copy(i, 0, 0).start()
     x_copy(0, 0).start()
-    for kind in (SECOND, NEXT):
-        for way in range(2):
-            z_copy(kind, way, 0).start()
+    for way in range(2):
+        z_copy(SECOND, way, 0).start()
     p_copy(0, 0, core).start()
 
     def arrive_z(kind, way):
@@ -178,20 +182,12 @@
 
     def arrive_x(o):
         x_copy(o, 1).wait_recv()
-        if o == 0:
-            for way in range(2):
-                z_copy(NEXT_B, way, 0).start()
         p_copy(1, o, core).start()
 
     def arrive_side():
         side_copy(1).wait_recv()
         for i in (2, 1, 3):
             col_copy(i, 1, 0).start()
-
-    arrive_side()
-    arrive_x(0)
-    for way in range(2):
-        arrive_z(NEXT, way)
 
     loads[2].wait()
     loads[3].wait()
@@ -205,8 +201,13 @@
     plan_copy = pltpu.make_async_copy(plan_v, plan, plan_sem.at[0])
     plan_copy.start()
 
+    arrive_side()
+    arrive_x(0)
     for way in range(2):
         arrive_z(SECOND, way)
+    for way in range(2):
+        z_copy(NEXT, way, 0).start()
+        z_copy(NEXT_B, way, 0).start()
 
     plan_copy.wait()
     for copy in tile_copies:
@@ -248,7 +249,6 @@
         def _():
             for way in range(2):
                 arrive_z(FOURTH, way)
-                arrive_z(NEXT_B, way)
 
         @pl.when(i == 5)
         def _():
@@ -269,15 +269,14 @@
         return 2 * rid(a, lax.rem(z + o, NZ), k)
 
     def extract(which, first, size):
-        def body(q, carry):
-            j = q // 2
-            rel = lax.rem(q, 2)
-            b = block_of(which, j, rel)
-            for blk in range(2):
-                part[which, j, rel, blk] = final_run(B_LAST, b + blk)
+        def body(j, carry):
+            for rel in range(2):
+                b = block_of(which, j, rel)
+                for blk in range(2):
+                    part[which, j, rel, blk] = final_run(B_LAST, b + blk)
             return carry
 
-        lax.fori_loop(2 * first, 2 * (first + size), body, 0)
+        lax.fori_loop(first, first + size, body, 0, unroll=True)
 
     def peer_copy(n):
         first, size = PIECES[n]
@@ -344,6 +343,9 @@
         for way in range(2):
             send_z(kind, way)
 
+    for way in range(2):
+        arrive_z(NEXT, way)
+        arrive_z(NEXT_B, way)
     for o in (3, 5, 4):
         arrive_x(o)
     for st in range(2):
@@ -359,35 +361,58 @@
                 acc = acc + jnp.dot(left, right, preferred_element_type=jnp.float32)
         return acc
 
-    term = lax.fori_loop(0, NZ, term_body, zero)
-    wt[...] = term.reshape(NCOL, F // NCOL, F)
+    term = lax.fori_loop(0, NZ, term_body, zero, unroll=True)
+    wt[...] = term.reshape(16, F // 16, F)
+
+    def near_slot(i, sign):
+        return crel(sign * (i // 2)) * 2 + flip(core, i)
+
+    def row_slot(i):
+        return flip(xh, i) * NZ + zrel(-(i // 2))
 
     def red1_copy(i):
-        return remote(wt.at[crel(i)], red1.at[i - 1], a1_s.at[i - 1], a1_r.at[i - 1], cpeer[i])
-
-    quad = xh * 2 + core
-    quad_peer = (None, partner, opposite, diagonal)
-
-    def quad_of(i):
-        k = core if i % 2 == 0 else 1 - core
-        return (xh if i < 2 else 1 - xh) * 2 + k
+        return remote(
+            wt.at[near_slot(i, 1)], red1.at[i - 1], a1_s.at[i - 1], a1_r.at[i - 1], near_peer[i]
+        )
 
     def red2_copy(i, owner):
         here = red2.at[owner]
-        return remote(here, here, a2_s.at[i - 1], a2_r.at[i - 1], quad_peer[i])
+        return remote(here, here, a2_s.at[i - 1], a2_r.at[i - 1], row_peer[i])
 
     def red3_copy(i, owner):
         here = red3.at[owner]
-        return remote(here, here, a3_s.at[i - 1], a3_r.at[i - 1], zpeer[i])
-
-    def red4_copy(i, owner):
-        here = red4.at[owner]
-        return remote(here, here, a4_s.at[i - 1], a4_r.at[i - 1], cpeer[i])
-
-    for i in (5, 3, 4, 6, 2, 7, 1):
+        return remote(here, here, a3_s.at[i - 1], a3_r.at[i - 1], near_peer[i])
+
+    for i in far:
         red1_copy(i).start()
 
-    lax.fori_loop(0, STEPS, lambda i, acc: tile_step(F_ORDER, i, acc, forward), zero)
+    def forward_body(i, acc):
+        @pl.when(i == 4)
+        def _():
+            for way in range(2):
+                send_z(FOURTH, way)
+
+        @pl.when(i == 6)
+        def _():
+            for way in range(2):
+                send_z(THIRD, way)
+
+        return tile_step(F_ORDER, i, acc, forward)
+
+    lax.fori_loop(0, STEPS, forward_body, zero)
+
+    for i in range(1, 16):
+        red1_copy(i).wait_recv()
+    total = wt[near_slot(0, 1)]
+    for i in range(15):
+        total = total + red1[i]
+    red2[row_slot(0)] = total
+    for i in far:
+        red2_copy(i, row_slot(0)).start()
+
+    for way in range(2):
+        rz_copy(NEXT_B, way).wait_recv()
+    send_x(0)
 
     for b in range(ROW_BLOCKS):
         agg[b] = final_run(F_LAST, b)
@@ -401,30 +426,17 @@
         agg_copy(i).start()
 
     for way in range(2):
-        send_z(FOURTH, way)
-    for way in range(2):
-        send_z(THIRD, way)
-    for way in range(2):
-        rz_copy(NEXT_B, way).wait_recv()
-    send_x(0)
-
-    for i in range(1, NCOL):
-        red1_copy(i).wait_recv()
-    total = wt[c]
-    for i in range(NCOL - 1):
-        total = total + red1[i]
-    red2[quad] = total
-    for i in (3, 2, 1):
-        red2_copy(i, quad).start()
-
-    for i in range(1, 4):
-        red2_copy(i, quad_of(i)).wait_recv()
-    red3[z] = red2[0] + red2[1] + red2[2] + red2[3]
-    for i in far_first:
-        red3_copy(i, z).start()
-
-    for way in range(2):
         send_z(SECOND, way)
+
+    for i in range(1, 16):
+        red2_copy(i, row_slot(i)).wait_recv()
+    total = red2[0]
+    for i in range(1, 16):
+        total = total + red2[i]
+    red3[near_slot(0, 1)] = total * (1.0 / math.sqrt(65536))
+    for i in far:
+        red3_copy(i, near_slot(0, 1)).start()
+
 
     for i in range(1, NCOL):
         agg_copy(i).wait_recv()
@@ -435,15 +447,6 @@
         lay_ref[blk] = jnp.dot(
             total.astype(jnp.bfloat16), w[...], preferred_element_type=jnp.float32
         ).astype(jnp.bfloat16)
-
-    for i in range(1, NZ):
-        red3_copy(i, zrel(-i)).wait_recv()
-    total = red3[0]
-    for i in range(1, NZ):
-        total = total + red3[i]
-    red4[c] = total * (1.0 / math.sqrt(65536))
-    for i in (5, 3, 4, 6, 2, 7, 1):
-        red4_copy(i, c).start()
 
     rx_copy(0).wait_recv()
     for kind in (NEXT, SECOND):
@@ -463,21 +466,20 @@
             )
         gf_ref[blk] = value.astype(jnp.bfloat16)
 
-    for i in range(1, NCOL):
-        red4_copy(i, crel(-i)).wait_recv()
-    gw_ref[...] = red4[...].reshape(F, F).T
+    for i in range(1, 16):
+        red3_copy(i, near_slot(i, -1)).wait_recv()
+    gw_ref[...] = red3[...].reshape(F, F).T
 
     side_copy(0).wait_send()
     for i in range(1, NCOL):
         agg_copy(i).wait_send()
-        red1_copy(i).wait_send()
-        red3_copy(i, z).wait_send()
-        red4_copy(i, c).wait_send()
     for near in range(2):
         for i in range(1, 4):
             col_copy(i, near, 0).wait_send()
-    for i in range(1, 4):
-        red2_copy(i, quad).wait_send()
+    for i in range(1, 16):
+        red1_copy(i).wait_send()
+        red2_copy(i, row_slot(0)).wait_send()
+        red3_copy(i, near_slot(0, 1)).wait_send()
     for n in range(len(PIECES)):
         peer_copy(n).wait_send()
     for kind in range(5):
@@ -492,21 +494,32 @@
             p_copy(st, o, core).wait_send()
 
 
+def hand_over(a, b, c, a_out, b_out, c_out, sem):
+    copies = [
+        pltpu.make_async_copy(src, dst, sem.at[i])
+        for i, (src, dst) in enumerate(((a, a_out), (b, b_out), (c, c_out)))
+    ]
+    for copy in copies:
+        copy.start()
+    for copy in copies:
+        copy.wait()
+
+
 def per_device(features, tiles, tile_rows, tile_cols, tile_count, weight, grad_out):
     bf, f32, i32 = jnp.bfloat16, jnp.float32, jnp.int32
     dma = pltpu.SemaphoreType.DMA
     vmem = pl.BlockSpec(memory_space=pltpu.VMEM)
-    anywhere = pl.BlockSpec(memory_space=pl.ANY)
+    hbm = pl.BlockSpec(memory_space=pltpu.HBM)
     pair = (2, TB, F)
     out_shape = (
         jax.ShapeDtypeStruct(pair, bf),
         jax.ShapeDtypeStruct(pair, bf),
         jax.ShapeDtypeStruct((F, F), f32),
     )
-    lay, gf, gw = pl.pallas_call(
+    made = pl.pallas_call(
         kernel,
         out_shape=out_shape,
-        in_specs=[pl.BlockSpec(memory_space=pltpu.SMEM)] + [anywhere] * 6,
+        in_specs=[pl.BlockSpec(memory_space=pltpu.SMEM)] + [hbm] * 6,
         out_specs=(vmem, vmem, vmem),
         scratch_shapes=[
             pltpu.VMEM((1, SLOTS), i32),
@@ -527,15 +540,14 @@
             pltpu.VMEM((5, 2, 2, F, TB), bf),
             pltpu.VMEM((ROW_BLOCKS, TB, F), bf),
             pltpu.VMEM((NCOL - 1, 2, TB, F), bf),
-            pltpu.VMEM((NCOL, F // NCOL, F), f32),
-            pltpu.VMEM((NCOL - 1, F // NCOL, F), f32),
-            pltpu.VMEM((4, F // NCOL, F), f32),
-            pltpu.VMEM((NZ, F // NCOL, F), f32),
-            pltpu.VMEM((NCOL, F // NCOL, F), f32),
+            pltpu.VMEM((16, F // 16, F), f32),
+            pltpu.VMEM((15, F // 16, F), f32),
+            pltpu.VMEM((16, F // 16, F), f32),
+            pltpu.VMEM((16, F // 16, F), f32),
             dma((5,)), dma((4,)), dma((1,)), dma((2, 4)), dma((2, 4)), dma((5, 2)), dma((5, 2)),
             dma((NZ,)), dma((NZ,)), dma((2, NZ)), dma((2, NZ)),
             dma((4,)), dma((4,)), dma((NZ,)), dma((NZ,)), dma((5, 2)), dma((5, 2)), dma((7,)), dma((7,)),
-            dma((7,)), dma((7,)), dma((3,)), dma((3,)), dma((7,)), dma((7,)), dma((7,)), dma((7,)),
+            dma((15,)), dma((15,)), dma((15,)), dma((15,)), dma((15,)), dma((15,)),
         ],
         compiler_params=pltpu.CompilerParams(
             collective_id=0, has_side_effects=True, vmem_limit_bytes=63 * 2**20
@@ -553,6 +565,14 @@
         weight,
         tiles.reshape(SLOTS, TB, TB),
     )
+    lay, gf, gw = pl.pallas_call(
+        hand_over,
+        out_shape=out_shape,
+        in_specs=[vmem] * 3,
+        out_specs=(hbm,) * 3,
+        scratch_shapes=[dma((3,))],
+        name="hand_over",
+    )(*made)
     return (lay.reshape(1, 2 * TB, F), gf.reshape(1, 2 * TB, F), gw)
 
 

time: 61.9 us -> 52.7 us (0.85)
  the two profiles are of different devices: /device:TPU:2 before, /device:TPU:1 now
where the time goes in v3:
time: 52.7 us; the launch traced here: 52.6 us
  Pallas kernels  51.3 us (97%)
  between operations  1.29 us (2%)
    pallas_call x1, Pallas kernels, per_device(): pl.pallas_call(kernel, out_shape=out_shape, in_specs=[pl.BlockSpec(memory...  49.7 us
    pallas_call x1, Pallas kernels, per_device(): pl.pallas_call(hand_over, out_shape=out_shape, in_specs=[vmem] * 3, out_s...  1.6 us

profile of v3, /device:TPU:1, one launch (start us, length us, event | category | flops | bytes accessed | tf_op | source)
XLA Modules:
  0.0 52.6 jit_solution(8075921517396097707)
XLA Ops:
  1.3 49.7 %aggregate.1 = (bf16[2,128,128]{2,1,0:T(8,128)(2,1)}, bf16[2,128,128]{2,1,0:T(8,128)(2,1)}, f32[128,128]{1,0:T(8,128)}) custom-call(s32[1,1]{1,0:T(1,128)S(6)} %copy.10.count, s32[1,256]{1,0:T(1,128)} %bitcast.10, s32[1,256]{1,0:T(1,128)} %bitcast.11, bf16[2,128,128]{2,1,0:T(8,128)(2,1)} %bitcast.8, bf16[2,128,128]{2,1,0:T(8,128)(2,1)} %bitcast.9, ...), custom_call_target="tpu_custom_call" | custom-call | flops 2147483648 | bytes 8388608 | tf_op jit(solution)/shard_map/aggregate/pallas_call | solution.py:519
  51.0 1.6 %hand_over.1 = (bf16[2,128,128]{2,1,0:T(8,128)(2,1)}, bf16[2,128,128]{2,1,0:T(8,128)(2,1)}, f32[128,128]{1,0:T(8,128)}) custom-call(bf16[2,128,128]{2,1,0:T(8,128)(2,1)} %get-tuple-element.9.a, bf16[2,128,128]{2,1,0:T(8,128)(2,1)} %get-tuple-element.10.b, f32[128,128]{1,0:T(8,128)} %get-tuple-element.11.c), custom_call_target="tpu_custom_call" | custom-call | tf_op jit(solution)/shard_map/hand_over/pallas_call | solution.py:568

commit v4 on v3

--- a/solution.py
+++ b/solution.py
@@ -51,9 +51,9 @@
 def kernel(
     count, rows_hbm, cols_hbm, feat_hbm, gout_hbm, w_hbm, tiles_hbm, lay_ref, gf_ref, gw_ref,
     rows, cols, gin, w, plan_v, plan,
-    tv, fbuf, gbuf, runs, part, peer, x_out, x_in, z_out, z_in,
+    tv, fbuf, gbuf, runs, part, peer, x_in, z_out, z_in,
     agg, agg_in, wt, red1, red2, red3,
-    load, tile_sem, plan_sem, col_s, col_r, agz_s, agz_r, agx_s, agx_r, agp_s, agp_r,
+    load, tile_sem, plan_sem, col_s, col_r, side_r, agz_s, agz_r, agx_s, agx_r, agp_s, agp_r,
     rp_s, rp_r, rx_s, rx_r, rz_s, rz_r, cr_s, cr_r,
     a1_s, a1_r, a2_s, a2_r, a3_s, a3_r,
 ):
@@ -89,6 +89,12 @@
     row_peer = [(rid(flip(xh, i), zrel(i // 2), core), c) for i in range(16)]
     zpeer = [None] + [(rid(xh, zrel(i), core), c) for i in range(1, NZ)]
     cpeer = [None] + [(r, crel(i)) for i in range(1, NCOL)]
+
+    def all_sent(like, sem):
+        remote(like, like, sem.at[0], sem.at[0], partner).wait_send()
+
+    def all_here(like, sem):
+        remote(like, like, sem.at[0], sem.at[0], partner).wait_recv()
 
     loads = [
         pltpu.make_async_copy(src, dst, load.at[i])
@@ -102,12 +108,7 @@
             )
         )
     ]
-    tile_copies = [
-        pltpu.make_async_copy(
-            tiles_hbm.at[pl.ds(64 * i, 64)], tv.at[pl.ds(64 * i, 64)], tile_sem.at[i]
-        )
-        for i in range(4)
-    ]
+    tile_copy = pltpu.make_async_copy(tiles_hbm, tv, tile_sem.at[0])
     barrier = pltpu.get_barrier_semaphore()
     everyone = [zpeer[i] for i in (1, 2, 6, 7)] + ypeer[1:] + [beside, opposite, partner]
     for device in everyone:
@@ -116,8 +117,7 @@
         )
     for copy in loads:
         copy.start()
-    for copy in tile_copies:
-        copy.start()
+    tile_copy.start()
     runs[EMPTY] = jnp.zeros((TB, F), jnp.float32)
     loads[0].wait()
     for blk in range(2):
@@ -130,11 +130,11 @@
 
     def col_copy(i, near, yo):
         here = col_shard(yo, near)
-        return remote(here, here, col_s.at[near, i], col_r.at[near, i], ypeer[i])
+        return remote(here, here, col_s.at[0], col_r.at[0], ypeer[i])
 
     def side_copy(near):
         here = col_shard(0, near)
-        return remote(here, here, col_s.at[0, 0], col_r.at[0, 0], beside)
+        return remote(here, here, col_s.at[0], side_r.at[0], beside)
 
     def shard(st, o, k):
         return fbuf.at[pl.ds(2 * rid(xh if st == 0 else 1 - xh, zrel(o), k), 2)]
@@ -146,16 +146,16 @@
             here = fbuf.at[pl.ds(2 * rid(xh, zrel(o), core) + way, 1)]
         step = 2 if kind in (SECOND, FOURTH) else 1
         return remote(
-            here, here, agz_s.at[kind, way], agz_r.at[kind, way], zpeer[(sign * step) % NZ]
+            here, here, agz_s.at[0], agz_r.at[kind, way], zpeer[(sign * step) % NZ]
         )
 
     def x_copy(o, st):
         here = shard(st, o, core)
-        return remote(here, here, agx_s.at[o % NZ], agx_r.at[o % NZ], opposite)
+        return remote(here, here, agx_s.at[0], agx_r.at[o % NZ], opposite)
 
     def p_copy(st, o, k):
         here = shard(st, o, k)
-        return remote(here, here, agp_s.at[st, o % NZ], agp_r.at[st, o % NZ], partner)
+        return remote(here, here, agp_s.at[0], agp_r.at[0], partner)
 
     side_copy(0).start()
     for i in (2, 1, 3):
@@ -210,12 +210,9 @@
         z_copy(NEXT_B, way, 0).start()
 
     plan_copy.wait()
-    for copy in tile_copies:
-        copy.wait()
+    tile_copy.wait()
     loads[4].wait()
-    for near in range(2):
-        for i in range(1, 4):
-            col_copy(i, near, -i).wait_recv()
+    all_here(gbuf.at[pl.ds(0, 12)], col_r)
 
     def tile_step(which, i, acc, product):
         value = [plan[which, i * UNROLL + u] for u in range(UNROLL)]
@@ -268,6 +265,8 @@
         a = jnp.where(rel == 1, xh, 1 - xh)
         return 2 * rid(a, lax.rem(z + o, NZ), k)
 
+    place = {o: j for j, o in enumerate(OFFSETS)}
+
     def extract(which, first, size):
         def body(j, carry):
             for rel in range(2):
@@ -282,11 +281,12 @@
         first, size = PIECES[n]
         return remote(
             part.at[0, pl.ds(first, size)], peer.at[pl.ds(first, size)],
-            rp_s.at[n], rp_r.at[n], partner,
+            rp_s.at[0], rp_r.at[n], partner,
         )
 
     def rx_copy(o):
-        return remote(x_out.at[o], x_in.at[o], rx_s.at[o], rx_r.at[o], opposite)
+        src = part.at[1, place[o], 0]
+        return remote(src, x_in.at[o], rx_s.at[0], rx_r.at[o], opposite)
 
     def rz_copy(kind, way):
         sign = 1 if way == 0 else -1
@@ -294,25 +294,28 @@
         if kind == FOURTH:
             src, dst = z_out.at[kind, way, way], z_in.at[kind, way, way]
         step = 2 if kind in (SECOND, FOURTH) else 1
-        return remote(src, dst, rz_s.at[kind, way], rz_r.at[kind, way], zpeer[(sign * step) % NZ])
+        return remote(src, dst, rz_s.at[0], rz_r.at[kind, way], zpeer[(sign * step) % NZ])
 
     def own(j, rel, blk):
-        return part[1, j, rel, blk].astype(jnp.float32) + peer[j, rel, blk].astype(jnp.float32)
+        return part[1, j, rel, blk].astype(jnp.float32)
 
     for n, (first, size) in enumerate(PIECES):
         extract(0, first, size)
         peer_copy(n).start()
     extract(1, 0, NZ)
-    place = {o: j for j, o in enumerate(OFFSETS)}
-
-    def send_x(o):
+    def pair_sum(j):
+        for rel in range(2):
+            for blk in range(2):
+                value = own(j, rel, blk) + peer[j, rel, blk].astype(jnp.float32)
+                part[1, j, rel, blk] = value.astype(jnp.bfloat16)
+
+    def send_x0():
         for blk in range(2):
-            value = own(place[o], 0, blk)
-            if o == 0:
-                for way in range(2):
-                    value = value + z_in[NEXT_B, way, blk].astype(jnp.float32)
-            x_out[o, blk] = value.astype(jnp.bfloat16)
-        rx_copy(o).start()
+            value = own(place[0], 0, blk)
+            for way in range(2):
+                value = value + z_in[NEXT_B, way, blk].astype(jnp.float32)
+            part[1, place[0], 0, blk] = value.astype(jnp.bfloat16)
+        rx_copy(0).start()
 
     def send_z(kind, way):
         o = (1, 2, 3, 4, 1)[kind] * (1 if way == 0 else -1) % NZ
@@ -337,8 +340,11 @@
 
     for n in range(len(PIECES)):
         peer_copy(n).wait_recv()
-        for o in ((4,), (3, 5), (2, 6), ())[n]:
-            send_x(o)
+        first, size = PIECES[n]
+        for j in range(first, first + size):
+            pair_sum(j)
+            if OFFSETS[j] in (2, 3, 4, 5, 6):
+                rx_copy(OFFSETS[j]).start()
     for kind in (NEXT_B, NEXT):
         for way in range(2):
             send_z(kind, way)
@@ -348,17 +354,12 @@
         arrive_z(NEXT_B, way)
     for o in (3, 5, 4):
         arrive_x(o)
-    for st in range(2):
-        for o in range(NZ):
-            p_copy(st, o, 1 - core).wait_recv()
-
     def term_body(j, acc):
-        for which in range(2):
-            for rel in range(2):
-                b = block_of(which, j, rel)
-                left = jnp.concatenate([part[which, j, rel, 0], part[which, j, rel, 1]], axis=1)
-                right = fbuf[pl.ds(b, 2)].reshape(2 * TB, F)
-                acc = acc + jnp.dot(left, right, preferred_element_type=jnp.float32)
+        for rel in range(2):
+            b = block_of(1, j, rel)
+            left = jnp.concatenate([part[1, j, rel, 0], part[1, j, rel, 1]], axis=1)
+            right = fbuf[pl.ds(b, 2)].reshape(2 * TB, F)
+            acc = acc + jnp.dot(left, right, preferred_element_type=jnp.float32)
         return acc
 
     term = lax.fori_loop(0, NZ, term_body, zero, unroll=True)
@@ -372,19 +373,21 @@
 
     def red1_copy(i):
         return remote(
-            wt.at[near_slot(i, 1)], red1.at[i - 1], a1_s.at[i - 1], a1_r.at[i - 1], near_peer[i]
+            wt.at[near_slot(i, 1)], red1.at[i - 1], a1_s.at[0], a1_r.at[0], near_peer[i]
         )
 
     def red2_copy(i, owner):
         here = red2.at[owner]
-        return remote(here, here, a2_s.at[i - 1], a2_r.at[i - 1], row_peer[i])
+        return remote(here, here, a2_s.at[0], a2_r.at[0], row_peer[i])
 
     def red3_copy(i, owner):
         here = red3.at[owner]
-        return remote(here, here, a3_s.at[i - 1], a3_r.at[i - 1], near_peer[i])
+        return remote(here, here, a3_s.at[0], a3_r.at[0], near_peer[i])
 
     for i in far:
         red1_copy(i).start()
+
+    all_here(fbuf.at[pl.ds(0, 32)], agp_r)
 
     def forward_body(i, acc):
         @pl.when(i == 4)
@@ -401,8 +404,7 @@
 
     lax.fori_loop(0, STEPS, forward_body, zero)
 
-    for i in range(1, 16):
-        red1_copy(i).wait_recv()
+    all_here(red1, a1_r)
     total = wt[near_slot(0, 1)]
     for i in range(15):
         total = total + red1[i]
@@ -412,14 +414,14 @@
 
     for way in range(2):
         rz_copy(NEXT_B, way).wait_recv()
-    send_x(0)
+    send_x0()
 
     for b in range(ROW_BLOCKS):
         agg[b] = final_run(F_LAST, b)
 
     def agg_copy(i):
         return remote(
-            agg.at[pl.ds(2 * crel(i), 2)], agg_in.at[i - 1], cr_s.at[i - 1], cr_r.at[i - 1], cpeer[i]
+            agg.at[pl.ds(2 * crel(i), 2)], agg_in.at[i - 1], cr_s.at[0], cr_r.at[0], cpeer[i]
         )
 
     for i in (5, 3, 4, 6, 2, 7, 1):
@@ -428,8 +430,7 @@
     for way in range(2):
         send_z(SECOND, way)
 
-    for i in range(1, 16):
-        red2_copy(i, row_slot(i)).wait_recv()
+    all_here(red2.at[pl.ds(0, 15)], a2_r)
     total = red2[0]
     for i in range(1, 16):
         total = total + red2[i]
@@ -438,8 +439,7 @@
         red3_copy(i, near_slot(0, 1)).start()
 
 
-    for i in range(1, NCOL):
-        agg_copy(i).wait_recv()
+    all_here(agg_in, cr_r)
     for blk in range(2):
         total = agg[2 * c + blk].astype(jnp.float32)
         for i in range(NCOL - 1):
@@ -466,32 +466,23 @@
             )
         gf_ref[blk] = value.astype(jnp.bfloat16)
 
-    for i in range(1, 16):
-        red3_copy(i, near_slot(i, -1)).wait_recv()
+    all_here(red3.at[pl.ds(0, 15)], a3_r)
     gw_ref[...] = red3[...].reshape(F, F).T
 
-    side_copy(0).wait_send()
-    for i in range(1, NCOL):
-        agg_copy(i).wait_send()
-    for near in range(2):
-        for i in range(1, 4):
-            col_copy(i, near, 0).wait_send()
-    for i in range(1, 16):
-        red1_copy(i).wait_send()
-        red2_copy(i, row_slot(0)).wait_send()
-        red3_copy(i, near_slot(0, 1)).wait_send()
-    for n in range(len(PIECES)):
-        peer_copy(n).wait_send()
-    for kind in range(5):
-        for way in range(2):
-            z_copy(kind, way, 0).wait_send()
-            rz_copy(kind, way).wait_send()
-    for o in (0, 2, 3, 4, 5, 6):
-        x_copy(o, 0).wait_send()
-        rx_copy(o).wait_send()
-    for st in range(2):
-        for o in range(NZ):
-            p_copy(st, o, core).wait_send()
+    for like, sem in (
+        (gbuf.at[pl.ds(0, 14)], col_s),
+        (fbuf.at[pl.ds(0, 18)], agz_s),
+        (fbuf.at[pl.ds(0, 12)], agx_s),
+        (fbuf.at[pl.ds(0, 32)], agp_s),
+        (part.at[0], rp_s),
+        (x_in.at[pl.ds(0, 6)], rx_s),
+        (fbuf.at[pl.ds(0, 18)], rz_s),
+        (agg_in, cr_s),
+        (red1, a1_s),
+        (red2.at[pl.ds(0, 15)], a2_s),
+        (red3.at[pl.ds(0, 15)], a3_s),
+    ):
+        all_sent(like, sem)
 
 
 def hand_over(a, b, c, a_out, b_out, c_out, sem):
@@ -535,7 +526,6 @@
             pltpu.VMEM((2, NZ, 2, 2, F, TB), bf),
             pltpu.VMEM((NZ, 2, 2, F, TB), bf),
             pltpu.VMEM((NZ, 2, F, TB), bf),
-            pltpu.VMEM((NZ, 2, F, TB), bf),
             pltpu.VMEM((5, 2, 2, F, TB), bf),
             pltpu.VMEM((5, 2, 2, F, TB), bf),
             pltpu.VMEM((ROW_BLOCKS, TB, F), bf),
@@ -544,10 +534,10 @@
             pltpu.VMEM((15, F // 16, F), f32),
             pltpu.VMEM((16, F // 16, F), f32),
             pltpu.VMEM((16, F // 16, F), f32),
-            dma((5,)), dma((4,)), dma((1,)), dma((2, 4)), dma((2, 4)), dma((5, 2)), dma((5, 2)),
-            dma((NZ,)), dma((NZ,)), dma((2, NZ)), dma((2, NZ)),
-            dma((4,)), dma((4,)), dma((NZ,)), dma((NZ,)), dma((5, 2)), dma((5, 2)), dma((7,)), dma((7,)),
-            dma((15,)), dma((15,)), dma((15,)), dma((15,)), dma((15,)), dma((15,)),
+            dma((5,)), dma((1,)), dma((1,)), dma((1,)), dma((1,)), dma((1,)),
+            dma((1,)), dma((5, 2)), dma((1,)), dma((NZ,)), dma((1,)), dma((1,)),
+            dma((1,)), dma((4,)), dma((1,)), dma((NZ,)), dma((1,)), dma((5, 2)), dma((1,)), dma((1,)),
+            dma((1,)), dma((1,)), dma((1,)), dma((1,)), dma((1,)), dma((1,)),
         ],
         compiler_params=pltpu.CompilerParams(
             collective_id=0, has_side_effects=True, vmem_limit_bytes=63 * 2**20

time: 52.7 us -> 51 us (0.968)
  Pallas kernels: 51.3 us -> 49.5 us
    pallas_call x1, Pallas kernels: 49.7 us -> 47.9 us  [per_device(): pl.pallas_call(kernel, out_shape=out_shape, in_specs=[pl.BlockSpec(memory...]
where the time goes in v4:
time: 51 us; the launch traced here: 50.8 us
  Pallas kernels  49.5 us (97%)
  between operations  1.29 us (3%)
    pallas_call x1, Pallas kernels, per_device(): pl.pallas_call(kernel, out_shape=out_shape, in_specs=[pl.BlockSpec(memory...  47.9 us
    pallas_call x1, Pallas kernels, per_device(): pl.pallas_call(hand_over, out_shape=out_shape, in_specs=[vmem] * 3, out_s...  1.6 us

profile of v4, /device:TPU:1, one launch (start us, length us, event | category | flops | bytes accessed | tf_op | source)
XLA Modules:
  0.0 50.8 jit_solution(12039988710883606572)
XLA Ops:
  1.3 47.9 %aggregate.1 = (bf16[2,128,128]{2,1,0:T(8,128)(2,1)}, bf16[2,128,128]{2,1,0:T(8,128)(2,1)}, f32[128,128]{1,0:T(8,128)}) custom-call(s32[1,1]{1,0:T(1,128)S(6)} %copy.10.count, s32[1,256]{1,0:T(1,128)} %bitcast.10, s32[1,256]{1,0:T(1,128)} %bitcast.11, bf16[2,128,128]{2,1,0:T(8,128)(2,1)} %bitcast.8, bf16[2,128,128]{2,1,0:T(8,128)(2,1)} %bitcast.9, ...), custom_call_target="tpu_custom_call" | custom-call | flops 2147483648 | bytes 8388608 | tf_op jit(solution)/shard_map/aggregate/pallas_call | solution.py:510
  49.2 1.6 %hand_over.1 = (bf16[2,128,128]{2,1,0:T(8,128)(2,1)}, bf16[2,128,128]{2,1,0:T(8,128)(2,1)}, f32[128,128]{1,0:T(8,128)}) custom-call(bf16[2,128,128]{2,1,0:T(8,128)(2,1)} %get-tuple-element.9.a, bf16[2,128,128]{2,1,0:T(8,128)(2,1)} %get-tuple-element.10.b, f32[128,128]{1,0:T(8,128)} %get-tuple-element.11.c), custom_call_target="tpu_custom_call" | custom-call | tf_op jit(solution)/shard_map/hand_over/pallas_call | solution.py:558

commit v5 on v4

--- a/solution.py
+++ b/solution.py
@@ -237,17 +237,17 @@
         return jnp.dot(tv[t], fbuf[o & (COL_BLOCKS - 1)], preferred_element_type=jnp.float32)
 
     def backward_body(i, acc):
-        @pl.when(i == 0)
+        @pl.when(i == 4)
         def _():
             for way in range(2):
                 arrive_z(THIRD, way)
 
-        @pl.when(i == 2)
+        @pl.when(i == 6)
         def _():
             for way in range(2):
                 arrive_z(FOURTH, way)
 
-        @pl.when(i == 5)
+        @pl.when(i == 7)
         def _():
             arrive_x(2)
             arrive_x(6)

time: 51 us -> 48.9 us (0.959)
  Pallas kernels: 49.5 us -> 47.5 us
    pallas_call x1, Pallas kernels: 47.9 us -> 45.9 us  [per_device(): pl.pallas_call(kernel, out_shape=out_shape, in_specs=[pl.BlockSpec(memory...]
where the time goes in v5:
time: 48.9 us; the launch traced here: 48.8 us
  Pallas kernels  47.5 us (97%)
  between operations  1.29 us (3%)
    pallas_call x1, Pallas kernels, per_device(): pl.pallas_call(kernel, out_shape=out_shape, in_specs=[pl.BlockSpec(memory...  45.9 us
    pallas_call x1, Pallas kernels, per_device(): pl.pallas_call(hand_over, out_shape=out_shape, in_specs=[vmem] * 3, out_s...  1.6 us

profile of v5, /device:TPU:1, one launch (start us, length us, event | category | flops | bytes accessed | tf_op | source)
XLA Modules:
  0.0 48.8 jit_solution(1175360323362727545)
XLA Ops:
  1.3 45.9 %aggregate.1 = (bf16[2,128,128]{2,1,0:T(8,128)(2,1)}, bf16[2,128,128]{2,1,0:T(8,128)(2,1)}, f32[128,128]{1,0:T(8,128)}) custom-call(s32[1,1]{1,0:T(1,128)S(6)} %copy.10.count, s32[1,256]{1,0:T(1,128)} %bitcast.10, s32[1,256]{1,0:T(1,128)} %bitcast.11, bf16[2,128,128]{2,1,0:T(8,128)(2,1)} %bitcast.8, bf16[2,128,128]{2,1,0:T(8,128)(2,1)} %bitcast.9, ...), custom_call_target="tpu_custom_call" | custom-call | flops 2147483648 | bytes 8388608 | tf_op jit(solution)/shard_map/aggregate/pallas_call | solution.py:510
  47.2 1.6 %hand_over.1 = (bf16[2,128,128]{2,1,0:T(8,128)(2,1)}, bf16[2,128,128]{2,1,0:T(8,128)(2,1)}, f32[128,128]{1,0:T(8,128)}) custom-call(bf16[2,128,128]{2,1,0:T(8,128)(2,1)} %get-tuple-element.9.a, bf16[2,128,128]{2,1,0:T(8,128)(2,1)} %get-tuple-element.10.b, f32[128,128]{1,0:T(8,128)} %get-tuple-element.11.c), custom_call_target="tpu_custom_call" | custom-call | tf_op jit(solution)/shard_map/hand_over/pallas_call | solution.py:558
